TPU v7x, 256 devices: a whole 4x4x8 slice. The times are simulated.
256 devices in a mesh: rows: 16 (over z, y_lo), cols: 16 (over y_hi, x, core).
Axes of the slice: x: 4, y: 4 (y_hi: 2, y_lo: 2; y = y_hi * 2 + y_lo), z: 8, core: 2. Of those that a mesh axis runs over, the one named last changes fastest.
Arguments:
- signal: float32 [32, 32, 64, 256], P(None, 'cols', 'rows'), may hold values from -6 to 6
- kernel: float32 [32, 32, 64, 256], P(None, 'cols', 'rows'), may hold values from -6 to 6
- gate_values: float32 [32, 32, 64, 256], P(None, 'cols', 'rows'), may hold values from -6 to 6
- grad_out: float32 [32, 32, 64, 256], P(None, 'cols', 'rows'), may hold values from -6 to 6
Outputs:
- gated: float32 [32, 32, 64, 256], P(None, 'cols', 'rows')
- signal_grad: float32 [32, 32, 64, 256], P(None, 'cols', 'rows')
- kernel_grad: float32 [32, 32, 64, 256], P(None, 'cols', 'rows')
- gate_grad: float32 [32, 32, 64, 256], P(None, 'cols', 'rows')
All inputs are finite; a program needn't handle non-finite values.
Results may differ from a plain program's by a relative error of at most 0.000098.
Values sent between devices are 32-bit elements; how exact they have to be, the bound alone decides.
No kernel may reach another device: no remote copies, remote signals or barrier semaphores. Data moves between devices by JAX's collectives and lax.ppermute only.
A program may use at most 64 MiB of HBM per device.

v0:
```python
import functools

import jax
import jax.numpy as jnp
import ml_dtypes
import numpy as np
from jax import lax
from jax.experimental import pallas as pl
from jax.experimental.pallas import tpu as pltpu
from jax.sharding import PartitionSpec as P

LENGTH = 65536
LANES = 128
FIELDS = 3
ROWS = 56
SCALE = 1.0 / (65536.0 * 256.0)
HALF = jnp.bfloat16


def halves(table):
    high = table.astype(np.float32).astype(ml_dtypes.bfloat16)
    low = (table - high.astype(np.float64)).astype(np.float32).astype(ml_dtypes.bfloat16)
    return high, low


@functools.lru_cache(maxsize=None)
def tables():
    a = np.arange(32)
    fa = np.arange(16)
    angle = 2.0 * np.pi * (fa[:, None] * a[None, :] % 32) / 32.0
    first = np.zeros((144, 128))
    last = np.zeros((144, 128))
    weight = np.where(fa == 0, 1.0, 2.0)[:, None] * SCALE
    for cl in range(4):
        columns = slice(32 * cl, 32 * cl + 32)
        first[16 * cl : 16 * cl + 16, columns] = np.cos(angle)
        first[64 + 16 * cl : 64 + 16 * cl + 16, columns] = -np.sin(angle)
        first[128 + cl, columns] = np.where(a % 2 == 0, 1.0, -1.0)
        last[16 * cl : 16 * cl + 16, columns] = weight * np.cos(angle)
        last[64 + 16 * cl : 64 + 16 * cl + 16, columns] = -weight * np.sin(angle)
        last[128 + cl, columns] = np.where(a % 2 == 0, SCALE, -SCALE)
    lane = np.arange(256)
    m = 16 * (lane % 16) + 8 * (lane // 128) + (lane // 16) % 8
    g0 = np.arange(256)
    middle = 2.0 * np.pi * (m[:, None] * g0[None, :] % 256) / 256.0
    forward = np.concatenate([np.cos(middle), np.sin(middle)], axis=1)
    backward = np.concatenate([np.cos(middle).T, np.sin(middle).T], axis=1)
    fa = np.arange(17)
    phase = 2.0 * np.pi * (8 * fa[:, None] * m[None, :] % LENGTH) / LENGTH
    turn_m = np.zeros((2, 24, 256), np.float32)
    turn_m[0, :17] = np.cos(phase)
    turn_m[1, :17] = np.sin(phase)
    c8 = np.arange(8)
    phase = c8[:, None, None] * (fa[None, :, None] + 32 * g0[None, None, :]) % LENGTH
    phase = 2.0 * np.pi * phase / LENGTH
    turn_c = np.zeros((2, 8, 24, 256), np.float32)
    turn_c[0, :, :17] = np.cos(phase)
    turn_c[1, :, :17] = np.sin(phase)
    return (*halves(first), *halves(forward), *halves(backward), *halves(last), turn_m, turn_c)


def split(values):
    high = values.astype(HALF)
    return high, (values - high.astype(jnp.float32)).astype(HALF)


def product(left, right, dims):
    def one(x, y):
        return lax.dot_general(x, y, (dims, ((), ())), preferred_element_type=jnp.float32)

    return one(left[0], right[0]) + (one(left[0], right[1]) + one(left[1], right[0]))


def eight(values, sign):
    def add(x, y):
        return (x[0] + y[0], x[1] + y[1])

    def sub(x, y):
        return (x[0] - y[0], x[1] - y[1])

    def quarter(x):
        return (-sign * x[1], sign * x[0])

    def four(v):
        s, d = add(v[0], v[2]), sub(v[0], v[2])
        t, u = add(v[1], v[3]), quarter(sub(v[1], v[3]))
        return [add(s, t), add(d, u), sub(s, t), sub(d, u)]

    root = float(np.sqrt(0.5))
    even, odd = four(values[0::2]), four(values[1::2])
    x = odd[1]
    odd[1] = (root * (x[0] - sign * x[1]), root * (x[1] + sign * x[0]))
    odd[2] = quarter(odd[2])
    x = odd[3]
    odd[3] = (root * (-x[0] - sign * x[1]), root * (-x[1] + sign * x[0]))
    return [add(x, y) for x, y in zip(even, odd)] + [sub(x, y) for x, y in zip(even, odd)]


def times(x, y):
    return (x[0] * y[0] - x[1] * y[1], x[0] * y[1] + x[1] * y[0])


def times_conj(x, y):
    return (x[0] * y[0] + x[1] * y[1], x[1] * y[0] - x[0] * y[1])


def pack_kernel(signal, kernel, gate, grad, out):
    for field in range(FIELDS):
        for half in range(2):
            for bl in range(2):
                parts = []
                for cl in range(4):
                    rows = pl.ds(bl * 8 + half * 4 + cl, 32, stride=16)
                    if field == 0:
                        parts.append(signal[rows, :])
                    elif field == 1:
                        parts.append(kernel[rows, :])
                    else:
                        parts.append(gate[rows, :] * grad[rows, :])
                block = jnp.concatenate(parts, axis=0).T
                out[pl.ds(half * 768 + field * 2 + bl, 128, stride=6), :] = block


def unpack_kernel(arrived, gate, grad, gated, signal_grad, kernel_grad, gate_grad):
    for field in range(FIELDS):
        for half in range(2):
            for bl in range(2):
                block = arrived[pl.ds(half * 768 + field * 2 + bl, 128, stride=6), :].T
                for cl in range(4):
                    rows = pl.ds(bl * 8 + half * 4 + cl, 32, stride=16)
                    part = block[32 * cl : 32 * cl + 32]
                    if field == 0:
                        gated[rows, :] = gate[rows, :] * part
                        gate_grad[rows, :] = grad[rows, :] * part
                    elif field == 1:
                        signal_grad[rows, :] = part
                    else:
                        kernel_grad[rows, :] = part


def channel_kernel(
    arrived, first_hi, first_lo, forward_hi, forward_lo, backward_hi, backward_lo,
    last_hi, last_lo, turn_m, turn_c, out, real, imag,
):
    pad = jnp.zeros((8, ROWS - 48, 256), jnp.float32)
    real[:, 48:ROWS, :] = pad
    imag[:, 48:ROWS, :] = pad
    cos_m, sin_m = turn_m[0, 0:16], turn_m[1, 0:16]
    cos_x, sin_x = turn_m[0, 16:17], turn_m[1, 16:17]
    first = (first_hi[...], first_lo[...])
    for field in range(FIELDS):
        blocks = [
            arrived[pl.ds(field * 2 + bl, 256, stride=6), :].reshape(8, 2, 16, 128) for bl in range(2)
        ]
        for e in range(2):
            block = jnp.concatenate([b[:, e].reshape(128, 128) for b in blocks], axis=0)
            mixed = product(first, split(block), ((1,), (1,)))
            for cl in range(4):
                c8 = 4 * e + cl
                x, y = mixed[16 * cl : 16 * cl + 16], mixed[64 + 16 * cl : 80 + 16 * cl]
                real[c8, 16 * field : 16 * field + 16, :] = x * cos_m + y * sin_m
                imag[c8, 16 * field : 16 * field + 16, :] = y * cos_m - x * sin_m
                x = mixed[128 + cl : 129 + cl]
                real[c8, 48 + field : 49 + field, :] = x * cos_x
                imag[c8, 48 + field : 49 + field, :] = -(x * sin_x)

    def along_lanes(table, sign):
        x = split(real[...].reshape(8 * ROWS, 256))
        y = split(imag[...].reshape(8 * ROWS, 256))
        x = product(x, table, ((1,), (0,)))
        y = product(y, table, ((1,), (0,)))
        real[...] = (x[:, :256] - sign * y[:, 256:]).reshape(8, ROWS, 256)
        imag[...] = (y[:, :256] + sign * x[:, 256:]).reshape(8, ROWS, 256)

    along_lanes((forward_hi[...], forward_lo[...]), -1.0)
    for rows_of, turns in (
        ([slice(16 * f, 16 * f + 8) for f in range(3)], slice(0, 8)),
        ([slice(16 * f + 8, 16 * f + 16) for f in range(3)], slice(8, 16)),
        ([slice(48 + f, 49 + f) for f in range(3)], slice(16, 17)),
    ):
        for lanes in (slice(0, 128), slice(128, 256)):
            turn = [(turn_c[0, c8, turns, lanes], turn_c[1, c8, turns, lanes]) for c8 in range(8)]
            spectra = []
            for rows in rows_of:
                values = [(real[c8, rows, lanes], imag[c8, rows, lanes]) for c8 in range(8)]
                spectra.append(eight([times_conj(v, t) for v, t in zip(values, turn)], -1.0))
            results = (
                [times(s, k) for s, k in zip(spectra[0], spectra[1])],
                [times_conj(g, k) for g, k in zip(spectra[2], spectra[1])],
                [times_conj(g, s) for g, s in zip(spectra[2], spectra[0])],
            )
            for rows, result in zip(rows_of, results):
                for c8, (v, t) in enumerate(zip(eight(result, 1.0), turn)):
                    v = times(v, t)
                    real[c8, rows, lanes] = v[0]
                    imag[c8, rows, lanes] = v[1]
    along_lanes((backward_hi[...], backward_lo[...]), 1.0)

    last = (last_hi[...], last_lo[...])
    fill = jnp.zeros((12, 256), jnp.float32)
    for field in range(FIELDS):
        done = []
        for e in range(2):
            reals, imags, extra = [], [], []
            for cl in range(4):
                c8 = 4 * e + cl
                x = real[c8, 16 * field : 16 * field + 16, :]
                y = imag[c8, 16 * field : 16 * field + 16, :]
                reals.append(x * cos_m - y * sin_m)
                imags.append(y * cos_m + x * sin_m)
                x, y = real[c8, 48 + field : 49 + field, :], imag[c8, 48 + field : 49 + field, :]
                extra.append(x * cos_x - y * sin_x)
            mixed = jnp.concatenate(reals + imags + extra + [fill], axis=0)
            done.append(product(split(mixed), last, ((0,), (0,))))
        for bl in range(2):
            pair = [d[128 * bl : 128 * bl + 128].reshape(8, 1, 16, 128) for d in done]
            block = jnp.concatenate(pair, axis=1).reshape(256, 128)
            out[pl.ds(field * 2 + bl, 256, stride=6), :] = block


VMEM = pl.BlockSpec(memory_space=pltpu.VMEM)


def call(body, operands, shapes, scratch=(), limit=32 << 20, flops=10**6):
    return pl.pallas_call(
        body,
        out_shape=shapes,
        in_specs=[VMEM] * len(operands),
        out_specs=jax.tree.map(lambda _: VMEM, shapes),
        scratch_shapes=scratch,
        compiler_params=pltpu.CompilerParams(vmem_limit_bytes=limit),
    )(*operands)


def flat(x):
    return x.reshape(32, 2, 4, 2, LANES).transpose(0, 1, 3, 2, 4).reshape(512, LANES)


def unflat(x):
    return x.reshape(32, 2, 2, 4, LANES).transpose(0, 1, 3, 2, 4).reshape(32, 2, 4, 256)


def exchange(x):
    x = x.reshape(256, FIELDS, 2, LANES)
    x = lax.all_to_all(x, ("rows", "cols"), split_axis=0, concat_axis=0, tiled=True)
    return x.reshape(256 * FIELDS * 2, LANES)


def shards(signal, kernel, gate_values, grad_out):
    signal, kernel, gate, grad = (flat(x) for x in (signal, kernel, gate_values, grad_out))
    wide = jax.ShapeDtypeStruct((1536, LANES), jnp.float32)
    own = jax.ShapeDtypeStruct((512, LANES), jnp.float32)
    packed = call(pack_kernel, (signal, kernel, gate, grad), wide)
    arrived = exchange(packed)
    scratch = [pltpu.VMEM((8, ROWS, 256), jnp.float32)] * 2
    done = call(channel_kernel, (arrived, *tables()), wide, scratch)
    results = call(unpack_kernel, (exchange(done), gate, grad), (own,) * 4)
    return tuple(unflat(x) for x in results)


def solution(mesh):
    place = P(None, "cols", "rows", None)
    return jax.shard_map(
        shards, mesh=mesh, in_specs=(place,) * 4, out_specs=(place,) * 4, check_vma=False
    )
```

profile of v0, /device:TPU:1, one launch (start us, length us, event | category | flops | bytes accessed | tf_op | source)
XLA Modules:
  0.0 85.0 jit_solution(15907880511956826190)
XLA Ops:
  0.6 0.0 copy-start
  0.6 0.9 %copy-done = f32[32,2,4,256]{3,2,1,0:T(4,128)S(1)} copy-done((f32[32,2,4,256]{3,2,1,0:T(4,128)S(1)}, f32[32,2,4,256]{3,2,1,0:T(4,128)}, u32[]{:S(2)}) %copy-start) | copy-done | bytes 262168
  1.6 0.0 copy-start.2
  1.6 0.9 %copy-done.2 = f32[32,2,4,256]{3,2,1,0:T(4,128)S(1)} copy-done((f32[32,2,4,256]{3,2,1,0:T(4,128)S(1)}, f32[32,2,4,256]{3,2,1,0:T(4,128)}, u32[]{:S(2)}) %copy-start.2) | copy-done | bytes 262168
  2.5 0.0 copy-start.5
  2.5 0.9 %copy-done.5 = f32[32,2,4,256]{3,2,1,0:T(4,128)S(1)} copy-done((f32[32,2,4,256]{3,2,1,0:T(4,128)S(1)}, f32[32,2,4,256]{3,2,1,0:T(4,128)}, u32[]{:S(2)}) %copy-start.5) | copy-done | bytes 262168
  3.5 0.0 copy-start.6
  3.5 0.9 %copy-done.6 = f32[32,2,4,256]{3,2,1,0:T(4,128)S(1)} copy-done((f32[32,2,4,256]{3,2,1,0:T(4,128)S(1)}, f32[32,2,4,256]{3,2,1,0:T(4,128)}, u32[]{:S(2)}) %copy-start.6) | copy-done | bytes 262168
  4.4 0.0 copy-start.14
  4.4 0.0 copy-start.15
  4.4 0.4 shard_map.165
  4.8 0.0 copy-start.4
  4.8 0.0 copy-start.7
  4.8 0.0 copy-start.8
  4.9 0.0 copy-start.9
  4.9 0.0 copy-start.10
  4.9 0.0 copy-start.11
  4.9 0.0 copy-start.12
  4.9 0.0 copy-start.13
  4.9 42.1 %all_to_all.10 = f32[256,3,2,128]{3,2,1,0:T(2,128)S(1)} all-to-all(f32[256,3,2,128]{3,2,1,0:T(2,128)S(1)} %bitcast.44), channel_id=1, replica_groups=mesh['rows'=16,'cols'=16] {'rows','cols'}, dimensions={0} | all-to-all | bytes 1572864 | tf_op jit(solution)/shard_map/all_to_all | solution.py:245
  47.0 0.0 copy-done.14
  47.0 0.0 copy-done.15
  47.1 0.0 copy-done.4
  47.1 0.0 copy-done.7
  47.1 0.0 copy-done.8
  47.1 0.0 copy-done.9
  47.1 0.0 copy-done.10
  47.1 0.0 copy-done.11
  47.1 0.0 copy-done.12
  47.1 0.0 copy-done.13
  47.1 3.7 %shard_map.166 = f32[1536,128]{1,0:T(8,128)S(1)} custom-call(f32[1536,128]{1,0:T(8,128)S(1)} %bitcast.46, bf16[144,128]{1,0:T(8,128)(2,1)S(1)} %copy-done.15, bf16[144,128]{1,0:T(8,128)(2,1)S(1)} %copy-done.14, bf16[256,512]{1,0:T(8,128)(2,1)S(1)} %copy-done.10, bf16[256,512]{1,0:T(8,128)(2,1)S(1)} %copy-done.9, bf16[256,512]{1,0:T(8,128)(2,1)S(1)} %copy-done.8, ...), custom_call_target="tpu_custom_call" | custom-call | tf_op jit(solution)/shard_map/pallas_call | solution.py:225
  50.8 0.0 copy-start.1
  50.8 0.0 copy-start.3
  50.8 32.8 %all_to_all.11 = f32[256,3,2,128]{3,2,1,0:T(2,128)S(1)} all-to-all(f32[256,3,2,128]{3,2,1,0:T(2,128)S(1)} %bitcast.47), channel_id=1, replica_groups=mesh['rows'=16,'cols'=16] {'rows','cols'}, dimensions={0} | all-to-all | bytes 1572864 | tf_op jit(solution)/shard_map/all_to_all | solution.py:245
  83.6 0.0 copy-done.1
  83.6 0.0 copy-done.3
  83.6 1.4 %shard_map.167 = (f32[512,128]{1,0:T(8,128)}, f32[512,128]{1,0:T(8,128)}, f32[512,128]{1,0:T(8,128)}, f32[512,128]{1,0:T(8,128)}) custom-call(f32[1536,128]{1,0:T(8,128)S(1)} %bitcast.45, f32[512,128]{1,0:T(8,128)S(1)} %bitcast.49, f32[512,128]{1,0:T(8,128)S(1)} %bitcast.51), custom_call_target="tpu_custom_call" | custom-call | tf_op jit(solution)/shard_map/pallas_call | solution.py:225
Async XLA Ops:
  0.6 1.0 %copy-start = (f32[32,2,4,256]{3,2,1,0:T(4,128)S(1)}, f32[32,2,4,256]{3,2,1,0:T(4,128)}, u32[]{:S(2)}) copy-start(f32[32,2,4,256]{3,2,1,0:T(4,128)} %param.16) | copy-start | bytes 786436
  1.6 0.9 %copy-start.2 = (f32[32,2,4,256]{3,2,1,0:T(4,128)S(1)}, f32[32,2,4,256]{3,2,1,0:T(4,128)}, u32[]{:S(2)}) copy-start(f32[32,2,4,256]{3,2,1,0:T(4,128)} %param.17) | copy-start | bytes 786436
  2.5 0.9 %copy-start.5 = (f32[32,2,4,256]{3,2,1,0:T(4,128)S(1)}, f32[32,2,4,256]{3,2,1,0:T(4,128)}, u32[]{:S(2)}) copy-start(f32[32,2,4,256]{3,2,1,0:T(4,128)} %param.14) | copy-start | bytes 786436
  3.5 0.9 %copy-start.6 = (f32[32,2,4,256]{3,2,1,0:T(4,128)S(1)}, f32[32,2,4,256]{3,2,1,0:T(4,128)}, u32[]{:S(2)}) copy-start(f32[32,2,4,256]{3,2,1,0:T(4,128)} %param.15) | copy-start | bytes 786436
  4.4 42.6 %copy-start.14 = (bf16[144,128]{1,0:T(8,128)(2,1)S(1)}, bf16[144,128]{1,0:T(8,128)(2,1)}, u32[]{:S(2)}) copy-start(bf16[144,128]{1,0:T(8,128)(2,1)} %constant.21.clone.first_lo) | copy-start | bytes 110596
  4.4 42.6 %copy-start.15 = (bf16[144,128]{1,0:T(8,128)(2,1)S(1)}, bf16[144,128]{1,0:T(8,128)(2,1)}, u32[]{:S(2)}) copy-start(bf16[144,128]{1,0:T(8,128)(2,1)} %constant.20.clone.first_hi) | copy-start | bytes 110596
  4.8 42.2 %copy-start.4 = (f32[2,8,24,256]{3,2,1,0:T(8,128)S(1)}, f32[2,8,24,256]{3,2,1,0:T(8,128)}, u32[]{:S(2)}) copy-start(f32[2,8,24,256]{3,2,1,0:T(8,128)} %constant.29.clone.turn_c) | copy-start | bytes 1179652
  4.8 42.2 %copy-start.7 = (bf16[256,512]{1,0:T(8,128)(2,1)S(1)}, bf16[256,512]{1,0:T(8,128)(2,1)}, u32[]{:S(2)}) copy-start(bf16[256,512]{1,0:T(8,128)(2,1)} %constant.25.clone.backward_lo) | copy-start | bytes 786436
  4.8 42.2 %copy-start.8 = (bf16[256,512]{1,0:T(8,128)(2,1)S(1)}, bf16[256,512]{1,0:T(8,128)(2,1)}, u32[]{:S(2)}) copy-start(bf16[256,512]{1,0:T(8,128)(2,1)} %constant.24.clone.backward_hi) | copy-start | bytes 786436
  4.9 42.2 %copy-start.9 = (bf16[256,512]{1,0:T(8,128)(2,1)S(1)}, bf16[256,512]{1,0:T(8,128)(2,1)}, u32[]{:S(2)}) copy-start(bf16[256,512]{1,0:T(8,128)(2,1)} %constant.23.clone.forward_lo) | copy-start | bytes 786436
  4.9 42.2 %copy-start.10 = (bf16[256,512]{1,0:T(8,128)(2,1)S(1)}, bf16[256,512]{1,0:T(8,128)(2,1)}, u32[]{:S(2)}) copy-start(bf16[256,512]{1,0:T(8,128)(2,1)} %constant.22.clone.forward_hi) | copy-start | bytes 786436
  4.9 42.2 %copy-start.11 = (f32[2,24,256]{2,1,0:T(8,128)S(1)}, f32[2,24,256]{2,1,0:T(8,128)}, u32[]{:S(2)}) copy-start(f32[2,24,256]{2,1,0:T(8,128)} %constant.28.clone.turn_m) | copy-start | bytes 147460
  4.9 42.2 %copy-start.12 = (bf16[144,128]{1,0:T(8,128)(2,1)S(1)}, bf16[144,128]{1,0:T(8,128)(2,1)}, u32[]{:S(2)}) copy-start(bf16[144,128]{1,0:T(8,128)(2,1)} %constant.27.clone.last_lo) | copy-start | bytes 110596
  4.9 42.2 %copy-start.13 = (bf16[144,128]{1,0:T(8,128)(2,1)S(1)}, bf16[144,128]{1,0:T(8,128)(2,1)}, u32[]{:S(2)}) copy-start(bf16[144,128]{1,0:T(8,128)(2,1)} %constant.26.clone.last_hi) | copy-start | bytes 110596
  50.8 32.8 %copy-start.1 = (f32[32,2,4,256]{3,2,1,0:T(4,128)S(1)}, f32[32,2,4,256]{3,2,1,0:T(4,128)}, u32[]{:S(2)}) copy-start(f32[32,2,4,256]{3,2,1,0:T(4,128)} %param.16) | copy-start | bytes 786436
  50.8 32.8 %copy-start.3 = (f32[32,2,4,256]{3,2,1,0:T(4,128)S(1)}, f32[32,2,4,256]{3,2,1,0:T(4,128)}, u32[]{:S(2)}) copy-start(f32[32,2,4,256]{3,2,1,0:T(4,128)} %param.17) | copy-start | bytes 786436
where the time goes:
time: 85.3 us; the launch traced here: 85 us
  blocking collectives  74.9 us (88%)
  Pallas kernels  5.46 us (6%)
  local copies, waits for them, and re-layouts  3.87 us (5%)
    all_to_all x2, blocking collectives, exchange(): lax.all_to_all(x, ('rows', 'cols'), split_axis=0, concat_axis=0, tiled=True)  74.9 us
    pallas_call x3, Pallas kernels, call(): pl.pallas_call(body, out_shape=shapes, in_specs=[VMEM] * len(operands), o...  5.46 us
    unnamed x32, local copies, waits for them, and re-layouts  3.87 us

commit v1 on v0

--- a/solution.py
+++ b/solution.py
@@ -21,6 +21,10 @@
     high = table.astype(np.float32).astype(ml_dtypes.bfloat16)
     low = (table - high.astype(np.float64)).astype(np.float32).astype(ml_dtypes.bfloat16)
     return high, low
+
+
+def tall(table):
+    return np.concatenate(np.split(table, 4, axis=1))
 
 
 @functools.lru_cache(maxsize=None)
@@ -56,7 +60,7 @@
     turn_c = np.zeros((2, 8, 24, 256), np.float32)
     turn_c[0, :, :17] = np.cos(phase)
     turn_c[1, :, :17] = np.sin(phase)
-    return (*halves(first), *halves(forward), *halves(backward), *halves(last), turn_m, turn_c)
+    return (*halves(first), *halves(tall(forward)), *halves(tall(backward)), *halves(last), turn_m, turn_c)
 
 
 def split(values):
@@ -104,28 +108,39 @@
     return (x[0] * y[0] + x[1] * y[1], x[1] * y[0] - x[0] * y[1])
 
 
-def pack_kernel(signal, kernel, gate, grad, out):
-    for field in range(FIELDS):
+def pack_kernel(signal, kernel, gate, grad, out, signal_v, kernel_v, gate_v, grad_v, done):
+    copies = []
+    for k, (source, target) in enumerate(
+        ((signal, signal_v), (kernel, kernel_v), (gate, gate_v), (grad, grad_v))
+    ):
+        for part in range(4):
+            rows = pl.ds(128 * part, 128)
+            copies.append(pltpu.make_async_copy(source.at[rows], target.at[rows], done.at[4 * k + part]))
+    for copy in copies:
+        copy.start()
+    for field in range(FIELDS):
+        for copy in copies[4 * field : 4 * field + 4] if field < 2 else copies[8:]:
+            copy.wait()
         for half in range(2):
             for bl in range(2):
                 parts = []
                 for cl in range(4):
                     rows = pl.ds(bl * 8 + half * 4 + cl, 32, stride=16)
                     if field == 0:
-                        parts.append(signal[rows, :])
+                        parts.append(signal_v[rows, :])
                     elif field == 1:
-                        parts.append(kernel[rows, :])
+                        parts.append(kernel_v[rows, :])
                     else:
-                        parts.append(gate[rows, :] * grad[rows, :])
+                        parts.append(gate_v[rows, :] * grad_v[rows, :])
                 block = jnp.concatenate(parts, axis=0).T
-                out[pl.ds(half * 768 + field * 2 + bl, 128, stride=6), :] = block
+                out[pl.ds(768 * half + field * 2 + bl, 128, stride=6), :] = block
 
 
 def unpack_kernel(arrived, gate, grad, gated, signal_grad, kernel_grad, gate_grad):
     for field in range(FIELDS):
-        for half in range(2):
-            for bl in range(2):
-                block = arrived[pl.ds(half * 768 + field * 2 + bl, 128, stride=6), :].T
+        for bl in range(2):
+            for half in range(2):
+                block = arrived[pl.ds(768 * half + field * 2 + bl, 128, stride=6), :].T
                 for cl in range(4):
                     rows = pl.ds(bl * 8 + half * 4 + cl, 32, stride=16)
                     part = block[32 * cl : 32 * cl + 32]
@@ -167,12 +182,13 @@
     def along_lanes(table, sign):
         x = split(real[...].reshape(8 * ROWS, 256))
         y = split(imag[...].reshape(8 * ROWS, 256))
+        table = [jnp.concatenate([t[256 * k : 256 * k + 256, :] for k in range(4)], axis=1) for t in table]
         x = product(x, table, ((1,), (0,)))
         y = product(y, table, ((1,), (0,)))
         real[...] = (x[:, :256] - sign * y[:, 256:]).reshape(8, ROWS, 256)
         imag[...] = (y[:, :256] + sign * x[:, 256:]).reshape(8, ROWS, 256)
 
-    along_lanes((forward_hi[...], forward_lo[...]), -1.0)
+    along_lanes((forward_hi, forward_lo), -1.0)
     for rows_of, turns in (
         ([slice(16 * f, 16 * f + 8) for f in range(3)], slice(0, 8)),
         ([slice(16 * f + 8, 16 * f + 16) for f in range(3)], slice(8, 16)),
@@ -194,7 +210,7 @@
                     v = times(v, t)
                     real[c8, rows, lanes] = v[0]
                     imag[c8, rows, lanes] = v[1]
-    along_lanes((backward_hi[...], backward_lo[...]), 1.0)
+    along_lanes((backward_hi, backward_lo), 1.0)
 
     last = (last_hi[...], last_lo[...])
     fill = jnp.zeros((12, 256), jnp.float32)
@@ -219,19 +235,40 @@
 
 
 VMEM = pl.BlockSpec(memory_space=pltpu.VMEM)
-
-
-def call(body, operands, shapes, scratch=(), limit=32 << 20, flops=10**6):
+HBM = pl.BlockSpec(memory_space=pltpu.HBM)
+
+
+def call(body, operands, in_specs, shapes, out_specs, scratch=(), limit=24 << 20):
     return pl.pallas_call(
         body,
         out_shape=shapes,
-        in_specs=[VMEM] * len(operands),
-        out_specs=jax.tree.map(lambda _: VMEM, shapes),
+        in_specs=in_specs,
+        out_specs=out_specs,
         scratch_shapes=scratch,
         compiler_params=pltpu.CompilerParams(vmem_limit_bytes=limit),
     )(*operands)
 
 
+WIDE = jax.ShapeDtypeStruct((1536, LANES), jnp.float32)
+OWN = jax.ShapeDtypeStruct((512, LANES), jnp.float32)
+WHOLE = [pltpu.VMEM((512, LANES), jnp.float32)] * 4 + [pltpu.SemaphoreType.DMA((16,))]
+
+
+def run_pack(signal, kernel, gate, grad):
+    return call(pack_kernel, (signal, kernel, gate, grad), [HBM] * 4, WIDE, VMEM, WHOLE)
+
+
+def run_channel(arrived):
+    constants = tables()
+    scratch = [pltpu.VMEM((8, ROWS, 256), jnp.float32)] * 2
+    specs = [VMEM] * (1 + len(constants))
+    return call(channel_kernel, (arrived, *constants), specs, WIDE, VMEM, scratch)
+
+
+def run_unpack(arrived, gate, grad):
+    return call(unpack_kernel, (arrived, gate, grad), [VMEM] * 3, (OWN,) * 4, (VMEM,) * 4)
+
+
 def flat(x):
     return x.reshape(32, 2, 4, 2, LANES).transpose(0, 1, 3, 2, 4).reshape(512, LANES)
 
@@ -243,19 +280,14 @@
 def exchange(x):
     x = x.reshape(256, FIELDS, 2, LANES)
     x = lax.all_to_all(x, ("rows", "cols"), split_axis=0, concat_axis=0, tiled=True)
-    return x.reshape(256 * FIELDS * 2, LANES)
+    return x.reshape(1536, LANES)
 
 
 def shards(signal, kernel, gate_values, grad_out):
-    signal, kernel, gate, grad = (flat(x) for x in (signal, kernel, gate_values, grad_out))
-    wide = jax.ShapeDtypeStruct((1536, LANES), jnp.float32)
-    own = jax.ShapeDtypeStruct((512, LANES), jnp.float32)
-    packed = call(pack_kernel, (signal, kernel, gate, grad), wide)
-    arrived = exchange(packed)
-    scratch = [pltpu.VMEM((8, ROWS, 256), jnp.float32)] * 2
-    done = call(channel_kernel, (arrived, *tables()), wide, scratch)
-    results = call(unpack_kernel, (exchange(done), gate, grad), (own,) * 4)
-    return tuple(unflat(x) for x in results)
+    inputs = [flat(x) for x in (signal, kernel, gate_values, grad_out)]
+    stored = [pltpu.with_memory_space_constraint(x, pltpu.HBM) for x in inputs]
+    done = exchange(run_channel(exchange(run_pack(*stored))))
+    return tuple(unflat(x) for x in run_unpack(done, *inputs[2:]))
 
 
 def solution(mesh):

time: 85.3 us -> 82.7 us (0.970)
  local copies, waits for them, and re-layouts: 3.87 us -> 0.08 us
  Pallas kernels: 5.46 us -> 6.7 us
    unnamed x32 -> x24, local copies, waits for them, and re-layouts: 3.87 us -> 0.08 us
    pallas_call x3, Pallas kernels: 5.46 us -> 6.7 us  [call(): pl.pallas_call(body, out_shape=shapes, in_specs=in_specs, out_specs=out_s...]
where the time goes in v1:
time: 82.7 us; the launch traced here: 82.5 us
  blocking collectives  74.9 us (91%)
  Pallas kernels  6.7 us (8%)
    all_to_all x2, blocking collectives, exchange(): lax.all_to_all(x, ('rows', 'cols'), split_axis=0, concat_axis=0, tiled=True)  74.9 us
    pallas_call x3, Pallas kernels, call(): pl.pallas_call(body, out_shape=shapes, in_specs=in_specs, out_specs=out_s...  6.7 us

profile of v1, /device:TPU:1, one launch (start us, length us, event | category | flops | bytes accessed | tf_op | source)
XLA Modules:
  0.0 82.5 jit_solution(6796758791076486056)
XLA Ops:
  0.6 0.0 copy-start.10
  0.6 0.0 copy-start.11
  0.7 1.6 %shard_map.165 = f32[1536,128]{1,0:T(8,128)S(1)} custom-call(f32[512,128]{1,0:T(8,128)} %bitcast.52, f32[512,128]{1,0:T(8,128)} %bitcast.53, f32[512,128]{1,0:T(8,128)} %bitcast.48, f32[512,128]{1,0:T(8,128)} %bitcast.50), custom_call_target="tpu_custom_call" | custom-call | tf_op jit(solution)/shard_map/pallas_call | solution.py:242
  2.3 0.0 copy-start.2
  2.3 0.0 copy-start.3
  2.3 0.0 copy-start.4
  2.3 0.0 copy-start.5
  2.3 0.0 copy-start.6
  2.3 0.0 copy-start.7
  2.3 0.0 copy-start.8
  2.3 0.0 copy-start.9
  2.4 42.1 %all_to_all.10 = f32[256,3,2,128]{3,2,1,0:T(2,128)S(1)} all-to-all(f32[256,3,2,128]{3,2,1,0:T(2,128)S(1)} %bitcast.44), channel_id=1, replica_groups=mesh['rows'=16,'cols'=16] {'rows','cols'}, dimensions={0} | all-to-all | bytes 1572864 | tf_op jit(solution)/shard_map/all_to_all | solution.py:282
  44.5 0.0 copy-done.10
  44.5 0.0 copy-done.11
  44.5 0.0 copy-done.2
  44.5 0.0 copy-done.3
  44.5 0.0 copy-done.4
  44.5 0.0 copy-done.5
  44.5 0.0 copy-done.6
  44.5 0.0 copy-done.7
  44.6 0.0 copy-done.8
  44.6 0.0 copy-done.9
  44.6 3.7 %shard_map.166 = f32[1536,128]{1,0:T(8,128)S(1)} custom-call(f32[1536,128]{1,0:T(8,128)S(1)} %bitcast.46, bf16[144,128]{1,0:T(8,128)(2,1)S(1)} %copy-done.11, bf16[144,128]{1,0:T(8,128)(2,1)S(1)} %copy-done.10, bf16[1024,128]{1,0:T(8,128)(2,1)S(1)} %copy-done.6, bf16[1024,128]{1,0:T(8,128)(2,1)S(1)} %copy-done.5, bf16[1024,128]{1,0:T(8,128)(2,1)S(1)} %copy-done.4, ...), custom_call_target="tpu_custom_call" | custom-call | tf_op jit(solution)/shard_map/pallas_call | solution.py:242
  48.3 0.0 copy-start
  48.3 0.0 copy-start.1
  48.3 32.7 %all_to_all.11 = f32[256,3,2,128]{3,2,1,0:T(2,128)S(1)} all-to-all(f32[256,3,2,128]{3,2,1,0:T(2,128)S(1)} %bitcast.47), channel_id=1, replica_groups=mesh['rows'=16,'cols'=16] {'rows','cols'}, dimensions={0} | all-to-all | bytes 1572864 | tf_op jit(solution)/shard_map/all_to_all | solution.py:282
  81.1 0.0 copy-done
  81.1 0.0 copy-done.1
  81.1 1.4 %shard_map.167 = (f32[512,128]{1,0:T(8,128)}, f32[512,128]{1,0:T(8,128)}, f32[512,128]{1,0:T(8,128)}, f32[512,128]{1,0:T(8,128)}) custom-call(f32[1536,128]{1,0:T(8,128)S(1)} %bitcast.45, f32[512,128]{1,0:T(8,128)S(1)} %bitcast.49, f32[512,128]{1,0:T(8,128)S(1)} %bitcast.51), custom_call_target="tpu_custom_call" | custom-call | tf_op jit(solution)/shard_map/pallas_call | solution.py:242
Async XLA Ops:
  0.6 43.9 %copy-start.10 = (bf16[144,128]{1,0:T(8,128)(2,1)S(1)}, bf16[144,128]{1,0:T(8,128)(2,1)}, u32[]{:S(2)}) copy-start(bf16[144,128]{1,0:T(8,128)(2,1)} %constant.21.clone.first_lo) | copy-start | bytes 110596
  0.6 43.9 %copy-start.11 = (bf16[144,128]{1,0:T(8,128)(2,1)S(1)}, bf16[144,128]{1,0:T(8,128)(2,1)}, u32[]{:S(2)}) copy-start(bf16[144,128]{1,0:T(8,128)(2,1)} %constant.20.clone.first_hi) | copy-start | bytes 110596
  2.3 42.2 %copy-start.2 = (f32[2,8,24,256]{3,2,1,0:T(8,128)S(1)}, f32[2,8,24,256]{3,2,1,0:T(8,128)}, u32[]{:S(2)}) copy-start(f32[2,8,24,256]{3,2,1,0:T(8,128)} %constant.29.clone.turn_c) | copy-start | bytes 1179652
  2.3 42.2 %copy-start.3 = (bf16[1024,128]{1,0:T(8,128)(2,1)S(1)}, bf16[1024,128]{1,0:T(8,128)(2,1)}, u32[]{:S(2)}) copy-start(bf16[1024,128]{1,0:T(8,128)(2,1)} %constant.25.clone.backward_lo) | copy-start | bytes 786436
  2.3 42.2 %copy-start.4 = (bf16[1024,128]{1,0:T(8,128)(2,1)S(1)}, bf16[1024,128]{1,0:T(8,128)(2,1)}, u32[]{:S(2)}) copy-start(bf16[1024,128]{1,0:T(8,128)(2,1)} %constant.24.clone.backward_hi) | copy-start | bytes 786436
  2.3 42.2 %copy-start.5 = (bf16[1024,128]{1,0:T(8,128)(2,1)S(1)}, bf16[1024,128]{1,0:T(8,128)(2,1)}, u32[]{:S(2)}) copy-start(bf16[1024,128]{1,0:T(8,128)(2,1)} %constant.23.clone.forward_lo) | copy-start | bytes 786436
  2.3 42.2 %copy-start.6 = (bf16[1024,128]{1,0:T(8,128)(2,1)S(1)}, bf16[1024,128]{1,0:T(8,128)(2,1)}, u32[]{:S(2)}) copy-start(bf16[1024,128]{1,0:T(8,128)(2,1)} %constant.22.clone.forward_hi) | copy-start | bytes 786436
  2.3 42.2 %copy-start.7 = (f32[2,24,256]{2,1,0:T(8,128)S(1)}, f32[2,24,256]{2,1,0:T(8,128)}, u32[]{:S(2)}) copy-start(f32[2,24,256]{2,1,0:T(8,128)} %constant.28.clone.turn_m) | copy-start | bytes 147460
  2.3 42.2 %copy-start.8 = (bf16[144,128]{1,0:T(8,128)(2,1)S(1)}, bf16[144,128]{1,0:T(8,128)(2,1)}, u32[]{:S(2)}) copy-start(bf16[144,128]{1,0:T(8,128)(2,1)} %constant.27.clone.last_lo) | copy-start | bytes 110596
  2.3 42.2 %copy-start.9 = (bf16[144,128]{1,0:T(8,128)(2,1)S(1)}, bf16[144,128]{1,0:T(8,128)(2,1)}, u32[]{:S(2)}) copy-start(bf16[144,128]{1,0:T(8,128)(2,1)} %constant.26.clone.last_hi) | copy-start | bytes 110596
  48.3 32.8 %copy-start = (f32[32,2,4,256]{3,2,1,0:T(4,128)S(1)}, f32[32,2,4,256]{3,2,1,0:T(4,128)}, u32[]{:S(2)}) copy-start(f32[32,2,4,256]{3,2,1,0:T(4,128)} %param.16) | copy-start | bytes 786436
  48.3 32.8 %copy-start.1 = (f32[32,2,4,256]{3,2,1,0:T(4,128)S(1)}, f32[32,2,4,256]{3,2,1,0:T(4,128)}, u32[]{:S(2)}) copy-start(f32[32,2,4,256]{3,2,1,0:T(4,128)} %param.17) | copy-start | bytes 786436

commit v2 on v1

v2 whole, which is shorter than its diff:
```python
import functools

import jax
import jax.numpy as jnp
import ml_dtypes
import numpy as np
from jax import lax
from jax.experimental import pallas as pl
from jax.experimental.pallas import tpu as pltpu
from jax.sharding import PartitionSpec as P

LENGTH = 65536
LANES = 128
FIELDS = 3
EXTRA = 384
ROWS = EXTRA + 32
SCALE = 1.0 / (65536.0 * 256.0)
HALF = jnp.bfloat16


def halves(table):
    high = table.astype(np.float32).astype(ml_dtypes.bfloat16)
    low = (table - high.astype(np.float64)).astype(np.float32).astype(ml_dtypes.bfloat16)
    return high, low


def tall(table):
    return np.concatenate(np.split(table, 4, axis=1))


@functools.lru_cache(maxsize=None)
def tables():
    a = np.arange(32)
    fa = np.arange(16)
    angle = 2.0 * np.pi * (fa[:, None] * a[None, :] % 32) / 32.0
    first = np.zeros((144, 128))
    last = np.zeros((128, 128))
    weight = np.where(fa == 0, 1.0, 2.0)[:, None] * SCALE
    for cl in range(4):
        columns = slice(32 * cl, 32 * cl + 32)
        first[16 * cl : 16 * cl + 16, columns] = np.cos(angle)
        first[64 + 16 * cl : 64 + 16 * cl + 16, columns] = -np.sin(angle)
        first[128 + cl, columns] = np.where(a % 2 == 0, 1.0, -1.0)
        last[16 * cl : 16 * cl + 16, columns] = weight * np.cos(angle)
        last[64 + 16 * cl : 64 + 16 * cl + 16, columns] = -weight * np.sin(angle)
        last[64 + 16 * cl, columns] = np.where(a % 2 == 0, SCALE, -SCALE)
    lane = np.arange(256)
    m = 16 * (lane % 16) + 8 * (lane // 128) + (lane // 16) % 8
    g0 = np.arange(256)
    middle = 2.0 * np.pi * (m[:, None] * g0[None, :] % 256) / 256.0
    forward = np.concatenate([np.cos(middle), np.sin(middle)], axis=1)
    backward = np.concatenate([np.cos(middle).T, np.sin(middle).T], axis=1)
    fa = np.arange(17)
    phase = 2.0 * np.pi * (8 * fa[:, None] * m[None, :] % LENGTH) / LENGTH
    turn_m = np.zeros((2, 24, 256), np.float32)
    turn_m[0, :17] = np.cos(phase)
    turn_m[1, :17] = np.sin(phase)
    c8 = np.arange(8)
    phase = c8[:, None, None] * (fa[None, :, None] + 32 * g0[None, None, :]) % LENGTH
    phase = 2.0 * np.pi * phase / LENGTH
    turn_c = np.zeros((2, 8, 24, 256), np.float32)
    turn_c[0, :, :17] = np.cos(phase)
    turn_c[1, :, :17] = np.sin(phase)
    return (*halves(first), *halves(tall(forward)), *halves(tall(backward)), turn_m, turn_c, *halves(last.T))


def split(values):
    high = values.astype(HALF)
    return high, (values - high.astype(jnp.float32)).astype(HALF)


def product(left, right, dims):
    def one(x, y):
        return lax.dot_general(x, y, (dims, ((), ())), preferred_element_type=jnp.float32)

    return one(left[0], right[0]) + (one(left[0], right[1]) + one(left[1], right[0]))


def eight(values, sign):
    def add(x, y):
        return (x[0] + y[0], x[1] + y[1])

    def sub(x, y):
        return (x[0] - y[0], x[1] - y[1])

    def quarter(x):
        return (-sign * x[1], sign * x[0])

    def four(v):
        s, d = add(v[0], v[2]), sub(v[0], v[2])
        t, u = add(v[1], v[3]), quarter(sub(v[1], v[3]))
        return [add(s, t), add(d, u), sub(s, t), sub(d, u)]

    root = float(np.sqrt(0.5))
    even, odd = four(values[0::2]), four(values[1::2])
    x = odd[1]
    odd[1] = (root * (x[0] - sign * x[1]), root * (x[1] + sign * x[0]))
    odd[2] = quarter(odd[2])
    x = odd[3]
    odd[3] = (root * (-x[0] - sign * x[1]), root * (-x[1] + sign * x[0]))
    return [add(x, y) for x, y in zip(even, odd)] + [sub(x, y) for x, y in zip(even, odd)]


def times(x, y):
    return (x[0] * y[0] - x[1] * y[1], x[0] * y[1] + x[1] * y[0])


def times_conj(x, y):
    return (x[0] * y[0] + x[1] * y[1], x[1] * y[0] - x[0] * y[1])


def pack_kernel(signal, kernel, gate, grad, out):
    for field in range(FIELDS):
        for half in range(2):
            for bl in range(2):
                parts = []
                for cl in range(4):
                    rows = pl.ds(bl * 8 + half * 4 + cl, 32, stride=16)
                    if field == 0:
                        parts.append(signal[rows, :])
                    elif field == 1:
                        parts.append(kernel[rows, :])
                    else:
                        parts.append(gate[rows, :] * grad[rows, :])
                block = jnp.concatenate(parts, axis=0).T
                out[pl.ds(768 * half + field * 2 + bl, 128, stride=6), :] = block


def unpack_kernel(arrived, last_hi, last_lo, gate, grad, gated, signal_grad, kernel_grad, gate_grad):
    last = (last_hi[...], last_lo[...])
    for field in range(FIELDS):
        for bl in range(2):
            block = arrived[pl.ds(field * 2 + bl, 256, stride=6), :]
            block = product(last, split(block), ((1,), (1,)))
            for half in range(2):
                for cl in range(4):
                    rows = pl.ds(bl * 8 + half * 4 + cl, 32, stride=16)
                    part = block[32 * cl : 32 * cl + 32, 128 * half : 128 * half + 128]
                    if field == 0:
                        gated[rows, :] = gate[rows, :] * part
                        gate_grad[rows, :] = grad[rows, :] * part
                    elif field == 1:
                        signal_grad[rows, :] = part
                    else:
                        kernel_grad[rows, :] = part


def channel_kernel(
    arrived, first_hi, first_lo, forward_hi, forward_lo, backward_hi, backward_lo, turn_m, turn_c,
    out, real, imag,
):
    cos_m, sin_m = turn_m[0, 0:16], turn_m[1, 0:16]
    cos_x, sin_x = turn_m[0, 16:17], turn_m[1, 16:17]
    first = (first_hi[...], first_lo[...])
    pad = jnp.zeros((8, 256), jnp.float32)
    real[EXTRA + 24 :, :] = pad
    imag[EXTRA + 24 :, :] = pad
    for field in range(FIELDS):
        blocks = [
            arrived[pl.ds(field * 2 + bl, 256, stride=6), :].reshape(8, 2, 16, 128) for bl in range(2)
        ]
        for e in range(2):
            block = jnp.concatenate([b[:, e].reshape(128, 128) for b in blocks], axis=0)
            mixed = product(first, split(block), ((1,), (1,)))
            for cl in range(4):
                rows = pl.ds(48 * (4 * e + cl) + 16 * field, 16)
                x, y = mixed[16 * cl : 16 * cl + 16], mixed[64 + 16 * cl : 80 + 16 * cl]
                real[rows, :] = x * cos_m + y * sin_m
                imag[rows, :] = y * cos_m - x * sin_m
            rows = pl.ds(EXTRA + 8 * field + 4 * e, 4)
            x = mixed[128:132]
            real[rows, :] = x * cos_x
            imag[rows, :] = -(x * sin_x)

    def along_lanes(refs, sign, source, target):
        table = [jnp.concatenate([ref[256 * k : 256 * k + 256, :] for k in range(4)], axis=1) for ref in refs]
        start = 0
        for size in (208, 208):
            rows = pl.ds(start, size)
            start += size
            x = product(split(source[0][rows, :]), table, ((1,), (0,)))
            y = product(split(source[1][rows, :]), table, ((1,), (0,)))
            if sign < 0:
                target[0][rows, :] = x[:, :256] + y[:, 256:]
                target[1][rows, :] = y[:, :256] - x[:, 256:]
            else:
                target[0][rows, :] = x[:, :256] - y[:, 256:]
                target[1][rows, :] = y[:, :256] + x[:, 256:]

    along_lanes((forward_hi, forward_lo), -1, (real, imag), (real, imag))
    for start, pitch, count, step, turns in (
        (0, 48, 8, 16, slice(0, 8)),
        (8, 48, 8, 16, slice(8, 16)),
        (EXTRA, 1, 1, 8, slice(16, 17)),
    ):
        for lanes in (slice(0, 128), slice(128, 256)):
            turn = [(turn_c[0, c8, turns, lanes], turn_c[1, c8, turns, lanes]) for c8 in range(8)]
            spectra = []
            for field in range(FIELDS):
                rows = [pl.ds(start + step * field + pitch * c8, count) for c8 in range(8)]
                values = [(real[r, lanes], imag[r, lanes]) for r in rows]
                spectra.append(eight([times_conj(v, t) for v, t in zip(values, turn)], -1.0))
            results = (
                [times(s, k) for s, k in zip(spectra[0], spectra[1])],
                [times_conj(g, k) for g, k in zip(spectra[2], spectra[1])],
                [times_conj(g, s) for g, s in zip(spectra[2], spectra[0])],
            )
            for field, result in enumerate(results):
                for c8, (v, t) in enumerate(zip(eight(result, 1.0), turn)):
                    rows = pl.ds(start + step * field + pitch * c8, count)
                    real[rows, lanes], imag[rows, lanes] = times(v, t)
    along_lanes((backward_hi, backward_lo), 1, (real, imag), (real, imag))

    lead = lax.broadcasted_iota(jnp.int32, (16, 256), 0) == 0
    for field in range(FIELDS):
        done = []
        for e in range(2):
            rows = pl.ds(EXTRA + 8 * field + 4 * e, 4)
            extra = real[rows, :] * cos_x - imag[rows, :] * sin_x
            reals, imags = [], []
            for cl in range(4):
                rows = pl.ds(48 * (4 * e + cl) + 16 * field, 16)
                x, y = real[rows, :], imag[rows, :]
                reals.append(x * cos_m - y * sin_m)
                imags.append(jnp.where(lead, extra[cl : cl + 1], y * cos_m + x * sin_m))
            done.append(jnp.concatenate(reals + imags, axis=0).T)
        for bl in range(2):
            pair = [d[128 * bl : 128 * bl + 128].reshape(8, 1, 16, 128) for d in done]
            block = jnp.concatenate(pair, axis=1).reshape(256, 128)
            out[pl.ds(field * 2 + bl, 256, stride=6), :] = block


VMEM = pl.BlockSpec(memory_space=pltpu.VMEM)


def call(body, operands, in_specs, shapes, out_specs, scratch=(), limit=24 << 20):
    return pl.pallas_call(
        body,
        out_shape=shapes,
        in_specs=in_specs,
        out_specs=out_specs,
        scratch_shapes=scratch,
        compiler_params=pltpu.CompilerParams(vmem_limit_bytes=limit),
    )(*operands)


WIDE = jax.ShapeDtypeStruct((1536, LANES), jnp.float32)
OWN = jax.ShapeDtypeStruct((512, LANES), jnp.float32)


def run_pack(signal, kernel, gate, grad):
    return call(pack_kernel, (signal, kernel, gate, grad), [VMEM] * 4, WIDE, VMEM)


def run_channel(arrived):
    constants = tables()[:-2]
    scratch = [pltpu.VMEM((ROWS, 256), jnp.float32)] * 2
    specs = [VMEM] * (1 + len(constants))
    return call(channel_kernel, (arrived, *constants), specs, WIDE, VMEM, scratch)


def run_unpack(arrived, gate, grad):
    operands = (arrived, *tables()[-2:], gate, grad)
    return call(unpack_kernel, operands, [VMEM] * 5, (OWN,) * 4, (VMEM,) * 4)


def flat(x):
    return x.reshape(32, 2, 4, 2, LANES).transpose(0, 1, 3, 2, 4).reshape(512, LANES)


def unflat(x):
    return x.reshape(32, 2, 2, 4, LANES).transpose(0, 1, 3, 2, 4).reshape(32, 2, 4, 256)


def exchange(x):
    x = x.reshape(256, FIELDS, 2, LANES)
    x = lax.all_to_all(x, ("rows", "cols"), split_axis=0, concat_axis=0, tiled=True)
    return x.reshape(1536, LANES)


def shards(signal, kernel, gate_values, grad_out):
    inputs = [flat(x) for x in (signal, kernel, gate_values, grad_out)]
    stored = [pltpu.with_memory_space_constraint(x, pltpu.HBM) for x in inputs]
    done = exchange(run_channel(exchange(run_pack(*stored))))
    return tuple(unflat(x) for x in run_unpack(done, *inputs[2:]))


def solution(mesh):
    place = P(None, "cols", "rows", None)
    return jax.shard_map(
        shards, mesh=mesh, in_specs=(place,) * 4, out_specs=(place,) * 4, check_vma=False
    )
```

time: 82.7 us -> 82 us (level)
  no operation moved by 1% of the time
where the time goes in v2:
time: 82 us; the launch traced here: 81.8 us
  blocking collectives  74.9 us (91%)
  Pallas kernels  6.1 us (7%)
    all_to_all x2, blocking collectives, exchange(): lax.all_to_all(x, ('rows', 'cols'), split_axis=0, concat_axis=0, tiled=True)  74.9 us
    pallas_call x3, Pallas kernels, call(): pl.pallas_call(body, out_shape=shapes, in_specs=in_specs, out_specs=out_s...  6.1 us

profile of v2, /device:TPU:1, one launch (start us, length us, event | category | flops | bytes accessed | tf_op | source)
XLA Modules:
  0.0 81.8 jit_solution(12260321994039954691)
XLA Ops:
  0.6 1.6 %shard_map.165 = f32[1536,128]{1,0:T(8,128)S(1)} custom-call(f32[512,128]{1,0:T(8,128)} %bitcast.52, f32[512,128]{1,0:T(8,128)} %bitcast.53, f32[512,128]{1,0:T(8,128)} %bitcast.48, f32[512,128]{1,0:T(8,128)} %bitcast.50), custom_call_target="tpu_custom_call" | custom-call | tf_op jit(solution)/shard_map/pallas_call | solution.py:237
  2.2 0.0 copy-start.2
  2.2 0.0 copy-start.3
  2.2 0.0 copy-start.4
  2.2 0.0 copy-start.5
  2.2 0.0 copy-start.6
  2.3 0.0 copy-start.7
  2.3 0.0 copy-start.8
  2.3 0.0 copy-start.9
  2.3 42.1 %all_to_all.10 = f32[256,3,2,128]{3,2,1,0:T(2,128)S(1)} all-to-all(f32[256,3,2,128]{3,2,1,0:T(2,128)S(1)} %bitcast.44), channel_id=1, replica_groups=mesh['rows'=16,'cols'=16] {'rows','cols'}, dimensions={0} | all-to-all | bytes 1572864 | tf_op jit(solution)/shard_map/all_to_all | solution.py:277
  44.4 0.0 copy-done.2
  44.4 0.0 copy-done.3
  44.4 0.0 copy-done.4
  44.4 0.0 copy-done.5
  44.5 0.0 copy-done.6
  44.5 0.0 copy-done.7
  44.5 0.0 copy-done.8
  44.5 0.0 copy-done.9
  44.5 3.0 %shard_map.166 = f32[1536,128]{1,0:T(8,128)S(1)} custom-call(f32[1536,128]{1,0:T(8,128)S(1)} %bitcast.45, bf16[144,128]{1,0:T(8,128)(2,1)S(1)} %copy-done.9, bf16[144,128]{1,0:T(8,128)(2,1)S(1)} %copy-done.8, bf16[1024,128]{1,0:T(8,128)(2,1)S(1)} %copy-done.6, bf16[1024,128]{1,0:T(8,128)(2,1)S(1)} %copy-done.5, bf16[1024,128]{1,0:T(8,128)(2,1)S(1)} %copy-done.4, ...), custom_call_target="tpu_custom_call" | custom-call | tf_op jit(solution)/shard_map/pallas_call | solution.py:237
  47.5 0.0 copy-start
  47.5 0.0 copy-start.1
  47.5 0.0 copy-start.10
  47.5 0.0 copy-start.11
  47.5 32.7 %all_to_all.11 = f32[256,3,2,128]{3,2,1,0:T(2,128)S(1)} all-to-all(f32[256,3,2,128]{3,2,1,0:T(2,128)S(1)} %bitcast.46), channel_id=1, replica_groups=mesh['rows'=16,'cols'=16] {'rows','cols'}, dimensions={0} | all-to-all | bytes 1572864 | tf_op jit(solution)/shard_map/all_to_all | solution.py:277
  80.3 0.0 copy-done
  80.3 0.0 copy-done.1
  80.3 0.0 copy-done.10
  80.3 0.0 copy-done.11
  80.3 1.5 %shard_map.167 = (f32[512,128]{1,0:T(8,128)}, f32[512,128]{1,0:T(8,128)}, f32[512,128]{1,0:T(8,128)}, f32[512,128]{1,0:T(8,128)}) custom-call(f32[1536,128]{1,0:T(8,128)S(1)} %bitcast.47, bf16[128,128]{1,0:T(8,128)(2,1)S(1)} %copy-done.11, bf16[128,128]{1,0:T(8,128)(2,1)S(1)} %copy-done.10, f32[512,128]{1,0:T(8,128)S(1)} %bitcast.49, f32[512,128]{1,0:T(8,128)S(1)} %bitcast.51), custom_call_target="tpu_custom_call" | custom-call | tf_op jit(solution)/shard_map/pallas_call | solution.py:237
Async XLA Ops:
  2.2 42.2 %copy-start.2 = (f32[2,8,24,256]{3,2,1,0:T(8,128)S(1)}, f32[2,8,24,256]{3,2,1,0:T(8,128)}, u32[]{:S(2)}) copy-start(f32[2,8,24,256]{3,2,1,0:T(8,128)} %constant.27.clone.turn_c) | copy-start | bytes 1179652
  2.2 42.2 %copy-start.3 = (bf16[1024,128]{1,0:T(8,128)(2,1)S(1)}, bf16[1024,128]{1,0:T(8,128)(2,1)}, u32[]{:S(2)}) copy-start(bf16[1024,128]{1,0:T(8,128)(2,1)} %constant.25.clone.backward_lo) | copy-start | bytes 786436
  2.2 42.2 %copy-start.4 = (bf16[1024,128]{1,0:T(8,128)(2,1)S(1)}, bf16[1024,128]{1,0:T(8,128)(2,1)}, u32[]{:S(2)}) copy-start(bf16[1024,128]{1,0:T(8,128)(2,1)} %constant.24.clone.backward_hi) | copy-start | bytes 786436
  2.2 42.2 %copy-start.5 = (bf16[1024,128]{1,0:T(8,128)(2,1)S(1)}, bf16[1024,128]{1,0:T(8,128)(2,1)}, u32[]{:S(2)}) copy-start(bf16[1024,128]{1,0:T(8,128)(2,1)} %constant.23.clone.forward_lo) | copy-start | bytes 786436
  2.2 42.2 %copy-start.6 = (bf16[1024,128]{1,0:T(8,128)(2,1)S(1)}, bf16[1024,128]{1,0:T(8,128)(2,1)}, u32[]{:S(2)}) copy-start(bf16[1024,128]{1,0:T(8,128)(2,1)} %constant.22.clone.forward_hi) | copy-start | bytes 786436
  2.3 42.2 %copy-start.7 = (f32[2,24,256]{2,1,0:T(8,128)S(1)}, f32[2,24,256]{2,1,0:T(8,128)}, u32[]{:S(2)}) copy-start(f32[2,24,256]{2,1,0:T(8,128)} %constant.26.clone.turn_m) | copy-start | bytes 147460
  2.3 42.2 %copy-start.8 = (bf16[144,128]{1,0:T(8,128)(2,1)S(1)}, bf16[144,128]{1,0:T(8,128)(2,1)}, u32[]{:S(2)}) copy-start(bf16[144,128]{1,0:T(8,128)(2,1)} %constant.21.clone.first_lo) | copy-start | bytes 110596
  2.3 42.2 %copy-start.9 = (bf16[144,128]{1,0:T(8,128)(2,1)S(1)}, bf16[144,128]{1,0:T(8,128)(2,1)}, u32[]{:S(2)}) copy-start(bf16[144,128]{1,0:T(8,128)(2,1)} %constant.20.clone.first_hi) | copy-start | bytes 110596
  47.5 32.8 %copy-start = (f32[32,2,4,256]{3,2,1,0:T(4,128)S(1)}, f32[32,2,4,256]{3,2,1,0:T(4,128)}, u32[]{:S(2)}) copy-start(f32[32,2,4,256]{3,2,1,0:T(4,128)} %param.16) | copy-start | bytes 786436
  47.5 32.8 %copy-start.1 = (f32[32,2,4,256]{3,2,1,0:T(4,128)S(1)}, f32[32,2,4,256]{3,2,1,0:T(4,128)}, u32[]{:S(2)}) copy-start(f32[32,2,4,256]{3,2,1,0:T(4,128)} %param.17) | copy-start | bytes 786436
  47.5 32.8 %copy-start.10 = (bf16[128,128]{1,0:T(8,128)(2,1)S(1)}, bf16[128,128]{1,0:T(8,128)(2,1)}, u32[]{:S(2)}) copy-start(bf16[128,128]{1,0:T(8,128)(2,1)} %constant.29.clone.last_lo) | copy-start | bytes 98308
  47.5 32.8 %copy-start.11 = (bf16[128,128]{1,0:T(8,128)(2,1)S(1)}, bf16[128,128]{1,0:T(8,128)(2,1)}, u32[]{:S(2)}) copy-start(bf16[128,128]{1,0:T(8,128)(2,1)} %constant.28.clone.last_hi) | copy-start | bytes 98308

commit v3 on v2

v3 whole, which is shorter than its diff:
```python
import functools

import jax
import jax.numpy as jnp
import ml_dtypes
import numpy as np
from jax import lax
from jax.experimental import pallas as pl
from jax.experimental.pallas import tpu as pltpu
from jax.sharding import PartitionSpec as P

LENGTH = 65536
LANES = 128
FIELDS = 3
EXTRA = 768
ROWS = EXTRA + 48
CHUNK = 448
SCALE = 1.0 / (65536.0 * 256.0)
HALF = jnp.bfloat16


def halves(table):
    high = table.astype(np.float32).astype(ml_dtypes.bfloat16)
    low = (table - high.astype(np.float64)).astype(np.float32).astype(ml_dtypes.bfloat16)
    return high, low


def tall(table):
    return np.concatenate(np.split(table, 2, axis=1))


@functools.lru_cache(maxsize=None)
def tables():
    a = np.arange(32)
    fa = np.arange(16)
    angle = 2.0 * np.pi * (fa[:, None] * a[None, :] % 32) / 32.0
    first = np.zeros((144, 128))
    last = np.zeros((128, 128))
    weight = np.where(fa == 0, 1.0, 2.0)[:, None] * SCALE
    for cl in range(4):
        columns = slice(32 * cl, 32 * cl + 32)
        first[16 * cl : 16 * cl + 16, columns] = np.cos(angle)
        first[64 + 16 * cl : 64 + 16 * cl + 16, columns] = -np.sin(angle)
        first[128 + cl, columns] = np.where(a % 2 == 0, 1.0, -1.0)
        last[16 * cl : 16 * cl + 16, columns] = weight * np.cos(angle)
        last[64 + 16 * cl : 64 + 16 * cl + 16, columns] = -weight * np.sin(angle)
        last[64 + 16 * cl, columns] = np.where(a % 2 == 0, SCALE, -SCALE)
    last = last.T.reshape(4, 32, 128)
    last = np.stack([np.kron([1.0, 0.0], last), np.kron([0.0, 1.0], last)]).transpose(2, 0, 1, 3).reshape(256, 256)
    lane = np.arange(128)
    m = 8 * (lane % 16) + 4 * (lane // 64) + (lane // 16) % 4
    g0 = np.arange(128)
    angle = 2.0 * np.pi * (m[:, None] * g0[None, :] % 128) / 128.0
    middle = np.block([[np.cos(angle), -np.sin(angle)], [np.sin(angle), np.cos(angle)]])
    c16 = np.arange(16)
    angle = 2.0 * np.pi * (c16[:, None] * c16[None, :] % 16) / 16.0
    cosine, sine = (np.kron(np.eye(FIELDS), part) for part in (np.cos(angle), np.sin(angle)))
    extra = np.block([[cosine, sine], [-sine, cosine]])
    fa = np.arange(17)
    phase = 2.0 * np.pi * (16 * fa[:, None] * m[None, :] % LENGTH) / LENGTH
    turn_m = np.zeros((2, 24, 128), np.float32)
    turn_m[0, :17] = np.cos(phase)
    turn_m[1, :17] = np.sin(phase)
    phase = c16[:, None, None] * (fa[None, :, None] + 32 * g0[None, None, :]) % LENGTH
    phase = 2.0 * np.pi * phase / LENGTH
    turn_c = np.stack([np.cos(phase), np.sin(phase)]).astype(np.float32)
    turn_x = np.tile(turn_c[:, :, 16], (1, FIELDS, 1))
    turn_c = np.ascontiguousarray(turn_c[:, :, :16])
    return (
        *halves(first), *halves(tall(middle)), *halves(extra), turn_m, turn_c, turn_x, *halves(tall(last))
    )


def split(values):
    high = values.astype(HALF)
    return high, (values - high.astype(jnp.float32)).astype(HALF)


def product(left, right, dims):
    def one(x, y):
        return lax.dot_general(x, y, (dims, ((), ())), preferred_element_type=jnp.float32)

    return one(left[0], right[0]) + (one(left[0], right[1]) + one(left[1], right[0]))


def sixteen(values, sign):
    def add(x, y):
        return (x[0] + y[0], x[1] + y[1])

    def sub(x, y):
        return (x[0] - y[0], x[1] - y[1])

    def quarter(x):
        return (-x[1], x[0]) if sign > 0 else (x[1], -x[0])

    def four(v):
        s, d = add(v[0], v[2]), sub(v[0], v[2])
        t, u = add(v[1], v[3]), quarter(sub(v[1], v[3]))
        return [add(s, t), add(d, u), sub(s, t), sub(d, u)]

    def turned(x, k):
        if k == 0:
            return x
        if k == 4:
            return quarter(x)
        cosine, sine = float(np.cos(np.pi * k / 8)), float(sign * np.sin(np.pi * k / 8))
        return (x[0] * cosine - x[1] * sine, x[0] * sine + x[1] * cosine)

    inner = [four(values[n::4]) for n in range(4)]
    outer = [four([turned(inner[n][k], n * k) for n in range(4)]) for k in range(4)]
    return [outer[k % 4][k // 4] for k in range(16)]


def times(x, y):
    return (x[0] * y[0] - x[1] * y[1], x[0] * y[1] + x[1] * y[0])


def times_conj(x, y):
    return (x[0] * y[0] + x[1] * y[1], x[1] * y[0] - x[0] * y[1])


def pack_kernel(signal, kernel, gate, grad, out):
    for field in range(FIELDS):
        for half in range(2):
            for bl in range(2):
                parts = []
                for cl in range(4):
                    rows = pl.ds(bl * 8 + half * 4 + cl, 32, stride=16)
                    if field == 0:
                        parts.append(signal[rows, :])
                    elif field == 1:
                        parts.append(kernel[rows, :])
                    else:
                        parts.append(gate[rows, :] * grad[rows, :])
                block = jnp.concatenate(parts, axis=0).T
                out[pl.ds(768 * half + field * 2 + bl, 128, stride=6), :] = block


def unpack_kernel(arrived, last_hi, last_lo, gate, grad, gated, signal_grad, kernel_grad, gate_grad):
    last = [jnp.concatenate([ref[0:256, :], ref[256:512, :]], axis=1) for ref in (last_hi, last_lo)]
    for field in range(FIELDS):
        block = [
            [arrived[pl.ds(768 * half + field * 2 + bl, 128, stride=6), :] for half in range(2)]
            for bl in range(2)
        ]
        block = jnp.concatenate([jnp.concatenate(b, axis=1) for b in block], axis=0)
        block = product(last, split(block), ((1,), (1,)))
        for a in range(32):
            for bl in range(2):
                rows = pl.ds(16 * a + 8 * bl, 8)
                part = block[8 * a : 8 * a + 8, 128 * bl : 128 * bl + 128]
                if field == 0:
                    gated[rows, :] = gate[rows, :] * part
                    gate_grad[rows, :] = grad[rows, :] * part
                elif field == 1:
                    signal_grad[rows, :] = part
                else:
                    kernel_grad[rows, :] = part


def channel_kernel(
    arrived, first_hi, first_lo, middle_hi, middle_lo, extra_hi, extra_lo, turn_m, turn_c, turn_x, out, data,
):
    re, im = slice(0, 128), slice(128, 256)
    cos_m, sin_m = turn_m[0, 0:16], turn_m[1, 0:16]
    cos_x, sin_x = turn_m[0, 16:17], turn_m[1, 16:17]
    first = (first_hi[...], first_lo[...])
    for field in range(FIELDS):
        blocks = [
            arrived[pl.ds(field * 2 + bl, 256, stride=6), :].reshape(4, 2, 2, 16, 128) for bl in range(2)
        ]
        for z0 in range(2):
            block = jnp.concatenate([b[:, z0, l].reshape(64, 128) for l in range(2) for b in blocks], axis=0)
            mixed = product(first, split(block), ((1,), (1,)))
            for l in range(2):
                lanes = slice(128 * l, 128 * l + 128)
                for cl in range(4):
                    rows = pl.ds(48 * (8 * z0 + 4 * l + cl) + 16 * field, 16)
                    x, y = mixed[16 * cl : 16 * cl + 16, lanes], mixed[64 + 16 * cl : 80 + 16 * cl, lanes]
                    data[rows, re] = x * cos_m + y * sin_m
                    data[rows, im] = y * cos_m - x * sin_m
                rows = pl.ds(EXTRA + 16 * field + 8 * z0 + 4 * l, 4)
                x = mixed[128:132, lanes]
                data[rows, re] = x * cos_x
                data[rows, im] = -(x * sin_x)

    middle = [jnp.concatenate([ref[0:256, :], ref[256:512, :]], axis=1) for ref in (middle_hi, middle_lo)]

    def along_lanes(dims):
        for start in range(0, ROWS, CHUNK):
            rows = pl.ds(start, min(CHUNK, ROWS - start))
            data[rows, :] = product(split(data[rows, :]), middle, dims)

    def multiply(spectra):
        signal, kernel, grad = spectra
        return (
            [times(s, k) for s, k in zip(signal, kernel)],
            [times_conj(g, k) for g, k in zip(grad, kernel)],
            [times_conj(g, s) for g, s in zip(grad, signal)],
        )

    along_lanes(((1,), (0,)))
    for start in (0, 8):
        turn = [(turn_c[0, c, start : start + 8], turn_c[1, c, start : start + 8]) for c in range(16)]
        spectra = []
        for field in range(FIELDS):
            rows = [pl.ds(start + 16 * field + 48 * c, 8) for c in range(16)]
            values = [times_conj((data[r, re], data[r, im]), t) for r, t in zip(rows, turn)]
            spectra.append(sixteen(values, -1))
        for field, result in enumerate(multiply(spectra)):
            for c, (v, t) in enumerate(zip(sixteen(result, 1), turn)):
                rows = pl.ds(start + 16 * field + 48 * c, 8)
                data[rows, re], data[rows, im] = times(v, t)
    rows, turn = pl.ds(EXTRA, 48), (turn_x[0], turn_x[1])
    extra = (extra_hi[...], extra_lo[...])
    values = jnp.concatenate(times_conj((data[rows, re], data[rows, im]), turn), axis=0)
    values = product(extra, split(values), ((1,), (0,)))
    spectra = [[(values[16 * f : 16 * f + 16], values[48 + 16 * f : 64 + 16 * f])] for f in range(FIELDS)]
    results = multiply(spectra)
    values = jnp.concatenate([result[0][part] for part in range(2) for result in results], axis=0)
    values = product(extra, split(values), ((0,), (0,)))
    data[rows, re], data[rows, im] = times((values[:48], values[48:]), turn)
    along_lanes(((1,), (1,)))

    lead = lax.broadcasted_iota(jnp.int32, (16, 128), 0) == 0
    for field in range(FIELDS):
        done = []
        for z0 in range(2):
            for l in range(2):
                rows = pl.ds(EXTRA + 16 * field + 8 * z0 + 4 * l, 4)
                extra = data[rows, re] * cos_x - data[rows, im] * sin_x
                reals, imags = [], []
                for cl in range(4):
                    rows = pl.ds(48 * (8 * z0 + 4 * l + cl) + 16 * field, 16)
                    x, y = data[rows, re], data[rows, im]
                    reals.append(x * cos_m - y * sin_m)
                    imags.append(jnp.where(lead, extra[cl : cl + 1], y * cos_m + x * sin_m))
                done.append(jnp.concatenate(reals + imags, axis=0).T)
        for bl in range(2):
            parts = [d[64 * bl : 64 * bl + 64].reshape(4, 1, 16, 128) for d in done]
            block = jnp.concatenate(parts, axis=1).reshape(256, 128)
            out[pl.ds(field * 2 + bl, 256, stride=6), :] = block


VMEM = pl.BlockSpec(memory_space=pltpu.VMEM)


def call(body, operands, in_specs, shapes, out_specs, scratch=(), limit=24 << 20):
    return pl.pallas_call(
        body,
        out_shape=shapes,
        in_specs=in_specs,
        out_specs=out_specs,
        scratch_shapes=scratch,
        compiler_params=pltpu.CompilerParams(vmem_limit_bytes=limit),
    )(*operands)


WIDE = jax.ShapeDtypeStruct((1536, LANES), jnp.float32)
OWN = jax.ShapeDtypeStruct((512, LANES), jnp.float32)


def run_pack(signal, kernel, gate, grad):
    return call(pack_kernel, (signal, kernel, gate, grad), [VMEM] * 4, WIDE, VMEM)


def run_channel(arrived):
    constants = tables()[:-2]
    scratch = [pltpu.VMEM((ROWS, 256), jnp.float32)]
    specs = [VMEM] * (1 + len(constants))
    return call(channel_kernel, (arrived, *constants), specs, WIDE, VMEM, scratch)


def run_unpack(arrived, gate, grad):
    operands = (arrived, *tables()[-2:], gate, grad)
    return call(unpack_kernel, operands, [VMEM] * 5, (OWN,) * 4, (VMEM,) * 4)


def flat(x):
    return x.reshape(32, 2, 4, 2, LANES).transpose(0, 1, 3, 2, 4).reshape(512, LANES)


def unflat(x):
    return x.reshape(32, 2, 2, 4, LANES).transpose(0, 1, 3, 2, 4).reshape(32, 2, 4, 256)


def exchange(x):
    x = x.reshape(256, FIELDS, 2, LANES)
    x = lax.all_to_all(x, ("rows", "cols"), split_axis=0, concat_axis=0, tiled=True)
    return x.reshape(1536, LANES)


def shards(signal, kernel, gate_values, grad_out):
    inputs = [flat(x) for x in (signal, kernel, gate_values, grad_out)]
    stored = [pltpu.with_memory_space_constraint(x, pltpu.HBM) for x in inputs]
    done = exchange(run_channel(exchange(run_pack(*stored))))
    return tuple(unflat(x) for x in run_unpack(done, *inputs[2:]))


def solution(mesh):
    place = P(None, "cols", "rows", None)
    return jax.shard_map(
        shards, mesh=mesh, in_specs=(place,) * 4, out_specs=(place,) * 4, check_vma=False
    )
```

time: 82 us -> 81.1 us (0.989)
  Pallas kernels: 6.1 us -> 5.14 us
    pallas_call x3, Pallas kernels: 6.1 us -> 5.14 us  [call(): pl.pallas_call(body, out_shape=shapes, in_specs=in_specs, out_specs=out_s...]
where the time goes in v3:
time: 81.1 us; the launch traced here: 80.9 us
  blocking collectives  74.9 us (92%)
  Pallas kernels  5.14 us (6%)
    all_to_all x2, blocking collectives, exchange(): lax.all_to_all(x, ('rows', 'cols'), split_axis=0, concat_axis=0, tiled=True)  74.9 us
    pallas_call x3, Pallas kernels, call(): pl.pallas_call(body, out_shape=shapes, in_specs=in_specs, out_specs=out_s...  5.14 us

profile of v3, /device:TPU:1, one launch (start us, length us, event | category | flops | bytes accessed | tf_op | source)
XLA Modules:
  0.0 80.9 jit_solution(11560335620942491494)
XLA Ops:
  0.6 1.6 %shard_map.174 = f32[1536,128]{1,0:T(8,128)S(1)} custom-call(f32[512,128]{1,0:T(8,128)} %bitcast.52, f32[512,128]{1,0:T(8,128)} %bitcast.53, f32[512,128]{1,0:T(8,128)} %bitcast.48, f32[512,128]{1,0:T(8,128)} %bitcast.50), custom_call_target="tpu_custom_call" | custom-call | tf_op jit(solution)/shard_map/pallas_call | solution.py:249
  2.2 0.0 copy-start.2
  2.2 0.0 copy-start.5
  2.2 0.0 copy-start.6
  2.2 0.0 copy-start.7
  2.2 0.0 copy-start.8
  2.3 0.0 copy-start.9
  2.3 0.0 copy-start.10
  2.3 0.0 copy-start.11
  2.3 0.0 copy-start.12
  2.3 42.1 %all_to_all.10 = f32[256,3,2,128]{3,2,1,0:T(2,128)S(1)} all-to-all(f32[256,3,2,128]{3,2,1,0:T(2,128)S(1)} %bitcast.44), channel_id=1, replica_groups=mesh['rows'=16,'cols'=16] {'rows','cols'}, dimensions={0} | all-to-all | bytes 1572864 | tf_op jit(solution)/shard_map/all_to_all | solution.py:289
  44.4 0.0 copy-done.2
  44.4 0.0 copy-done.5
  44.4 0.0 copy-done.6
  44.5 0.0 copy-done.7
  44.5 0.0 copy-done.8
  44.5 0.0 copy-done.9
  44.5 0.0 copy-done.10
  44.5 0.0 copy-done.11
  44.5 0.0 copy-done.12
  44.5 2.3 %shard_map.175 = f32[1536,128]{1,0:T(8,128)S(1)} custom-call(f32[1536,128]{1,0:T(8,128)S(1)} %bitcast.45, bf16[144,128]{1,0:T(8,128)(2,1)S(1)} %copy-done.9, bf16[144,128]{1,0:T(8,128)(2,1)S(1)} %copy-done.8, bf16[512,128]{1,0:T(8,128)(2,1)S(1)} %copy-done.6, bf16[512,128]{1,0:T(8,128)(2,1)S(1)} %copy-done.5, bf16[96,96]{1,0:T(8,128)(2,1)S(1)} %copy-done.12, ...), custom_call_target="tpu_custom_call" | custom-call | tf_op jit(solution)/shard_map/pallas_call | solution.py:249
  46.8 0.0 copy-start
  46.8 0.0 copy-start.1
  46.8 0.0 copy-start.3
  46.8 0.0 copy-start.4
  46.8 32.8 %all_to_all.11 = f32[256,3,2,128]{3,2,1,0:T(2,128)S(1)} all-to-all(f32[256,3,2,128]{3,2,1,0:T(2,128)S(1)} %bitcast.46), channel_id=1, replica_groups=mesh['rows'=16,'cols'=16] {'rows','cols'}, dimensions={0} | all-to-all | bytes 1572864 | tf_op jit(solution)/shard_map/all_to_all | solution.py:289
  79.6 0.0 copy-done
  79.6 0.0 copy-done.1
  79.6 0.0 copy-done.3
  79.6 0.0 copy-done.4
  79.6 1.3 %shard_map.176 = (f32[512,128]{1,0:T(8,128)}, f32[512,128]{1,0:T(8,128)}, f32[512,128]{1,0:T(8,128)}, f32[512,128]{1,0:T(8,128)}) custom-call(f32[1536,128]{1,0:T(8,128)S(1)} %bitcast.47, bf16[512,128]{1,0:T(8,128)(2,1)S(1)} %copy-done.4, bf16[512,128]{1,0:T(8,128)(2,1)S(1)} %copy-done.3, f32[512,128]{1,0:T(8,128)S(1)} %bitcast.49, f32[512,128]{1,0:T(8,128)S(1)} %bitcast.51), custom_call_target="tpu_custom_call" | custom-call | tf_op jit(solution)/shard_map/pallas_call | solution.py:249
Async XLA Ops:
  2.2 42.2 %copy-start.2 = (f32[2,16,16,128]{3,2,1,0:T(8,128)S(1)}, f32[2,16,16,128]{3,2,1,0:T(8,128)}, u32[]{:S(2)}) copy-start(f32[2,16,16,128]{3,2,1,0:T(8,128)} %constant.29.clone.turn_c) | copy-start | bytes 786436
  2.2 42.2 %copy-start.5 = (bf16[512,128]{1,0:T(8,128)(2,1)S(1)}, bf16[512,128]{1,0:T(8,128)(2,1)}, u32[]{:S(2)}) copy-start(bf16[512,128]{1,0:T(8,128)(2,1)} %constant.25.clone.middle_lo) | copy-start | bytes 393220
  2.2 42.2 %copy-start.6 = (bf16[512,128]{1,0:T(8,128)(2,1)S(1)}, bf16[512,128]{1,0:T(8,128)(2,1)}, u32[]{:S(2)}) copy-start(bf16[512,128]{1,0:T(8,128)(2,1)} %constant.24.clone.middle_hi) | copy-start | bytes 393220
  2.2 42.2 %copy-start.7 = (f32[2,48,128]{2,1,0:T(8,128)S(1)}, f32[2,48,128]{2,1,0:T(8,128)}, u32[]{:S(2)}) copy-start(f32[2,48,128]{2,1,0:T(8,128)} %constant.30.clone.turn_x) | copy-start | bytes 147460
  2.2 42.2 %copy-start.8 = (bf16[144,128]{1,0:T(8,128)(2,1)S(1)}, bf16[144,128]{1,0:T(8,128)(2,1)}, u32[]{:S(2)}) copy-start(bf16[144,128]{1,0:T(8,128)(2,1)} %constant.23.clone.first_lo) | copy-start | bytes 110596
  2.3 42.2 %copy-start.9 = (bf16[144,128]{1,0:T(8,128)(2,1)S(1)}, bf16[144,128]{1,0:T(8,128)(2,1)}, u32[]{:S(2)}) copy-start(bf16[144,128]{1,0:T(8,128)(2,1)} %constant.22.clone.first_hi) | copy-start | bytes 110596
  2.3 42.2 %copy-start.10 = (f32[2,24,128]{2,1,0:T(8,128)S(1)}, f32[2,24,128]{2,1,0:T(8,128)}, u32[]{:S(2)}) copy-start(f32[2,24,128]{2,1,0:T(8,128)} %constant.28.clone.turn_m) | copy-start | bytes 73732
  2.3 42.2 %copy-start.11 = (bf16[96,96]{1,0:T(8,128)(2,1)S(1)}, bf16[96,96]{1,0:T(8,128)(2,1)}, u32[]{:S(2)}) copy-start(bf16[96,96]{1,0:T(8,128)(2,1)} %constant.27.clone.extra_lo) | copy-start | bytes 55300
  2.3 42.2 %copy-start.12 = (bf16[96,96]{1,0:T(8,128)(2,1)S(1)}, bf16[96,96]{1,0:T(8,128)(2,1)}, u32[]{:S(2)}) copy-start(bf16[96,96]{1,0:T(8,128)(2,1)} %constant.26.clone.extra_hi) | copy-start | bytes 55300
  46.8 32.8 %copy-start = (f32[32,2,4,256]{3,2,1,0:T(4,128)S(1)}, f32[32,2,4,256]{3,2,1,0:T(4,128)}, u32[]{:S(2)}) copy-start(f32[32,2,4,256]{3,2,1,0:T(4,128)} %param.17) | copy-start | bytes 786436
  46.8 32.8 %copy-start.1 = (f32[32,2,4,256]{3,2,1,0:T(4,128)S(1)}, f32[32,2,4,256]{3,2,1,0:T(4,128)}, u32[]{:S(2)}) copy-start(f32[32,2,4,256]{3,2,1,0:T(4,128)} %param.18) | copy-start | bytes 786436
  46.8 32.8 %copy-start.3 = (bf16[512,128]{1,0:T(8,128)(2,1)S(1)}, bf16[512,128]{1,0:T(8,128)(2,1)}, u32[]{:S(2)}) copy-start(bf16[512,128]{1,0:T(8,128)(2,1)} %constant.32.clone.last_lo) | copy-start | bytes 393220
  46.8 32.8 %copy-start.4 = (bf16[512,128]{1,0:T(8,128)(2,1)S(1)}, bf16[512,128]{1,0:T(8,128)(2,1)}, u32[]{:S(2)}) copy-start(bf16[512,128]{1,0:T(8,128)(2,1)} %constant.31.clone.last_hi) | copy-start | bytes 393220

commit v4 on v3

--- a/solution.py
+++ b/solution.py
@@ -10,6 +10,14 @@
 from jax.sharding import PartitionSpec as P
 
 LENGTH = 65536
+LISTED = [
+    (2 * z + l) * 16 + 8 * h + 2 * x + core
+    for z in range(8)
+    for core in range(2)
+    for x in range(4)
+    for h in range(2)
+    for l in range(2)
+]
 LANES = 128
 FIELDS = 3
 EXTRA = 768
@@ -47,8 +55,10 @@
         last[64 + 16 * cl, columns] = np.where(a % 2 == 0, SCALE, -SCALE)
     last = last.T.reshape(4, 32, 128)
     last = np.stack([np.kron([1.0, 0.0], last), np.kron([0.0, 1.0], last)]).transpose(2, 0, 1, 3).reshape(256, 256)
+    first = first.reshape(144, 4, 2, 16).transpose(0, 3, 2, 1).reshape(144, 128)
     lane = np.arange(128)
-    m = 8 * (lane % 16) + 4 * (lane // 64) + (lane // 16) % 4
+    q = 8 * (lane % 2) + 2 * (lane // 2 % 4) + lane // 8 % 2
+    m = 8 * q + 4 * (lane // 64) + lane // 16 % 4
     g0 = np.arange(128)
     angle = 2.0 * np.pi * (m[:, None] * g0[None, :] % 128) / 128.0
     middle = np.block([[np.cos(angle), -np.sin(angle)], [np.sin(angle), np.cos(angle)]])
@@ -121,19 +131,13 @@
 
 def pack_kernel(signal, kernel, gate, grad, out):
     for field in range(FIELDS):
+        block = signal[...] if field == 0 else kernel[...] if field == 1 else gate[...] * grad[...]
+        block = block.reshape(2, 16, 2, 8, 128)
         for half in range(2):
             for bl in range(2):
-                parts = []
-                for cl in range(4):
-                    rows = pl.ds(bl * 8 + half * 4 + cl, 32, stride=16)
-                    if field == 0:
-                        parts.append(signal[rows, :])
-                    elif field == 1:
-                        parts.append(kernel[rows, :])
-                    else:
-                        parts.append(gate[rows, :] * grad[rows, :])
-                block = jnp.concatenate(parts, axis=0).T
-                out[pl.ds(768 * half + field * 2 + bl, 128, stride=6), :] = block
+                parts = [block[k, :, bl, 4 * half : 4 * half + 4] for k in range(2)]
+                part = jnp.concatenate(parts, axis=1).reshape(128, 128)
+                out[pl.ds(768 * half + field * 2 + bl, 128, stride=6), :] = part.T
 
 
 def unpack_kernel(arrived, last_hi, last_lo, gate, grad, gated, signal_grad, kernel_grad, gate_grad):
@@ -167,10 +171,12 @@
     first = (first_hi[...], first_lo[...])
     for field in range(FIELDS):
         blocks = [
-            arrived[pl.ds(field * 2 + bl, 256, stride=6), :].reshape(4, 2, 2, 16, 128) for bl in range(2)
+            arrived[pl.ds(6 * l + field * 2 + bl, 128, stride=12), :].reshape(4, 2, 16, 128)
+            for l in range(2)
+            for bl in range(2)
         ]
         for z0 in range(2):
-            block = jnp.concatenate([b[:, z0, l].reshape(64, 128) for l in range(2) for b in blocks], axis=0)
+            block = jnp.concatenate([b[:, z0].reshape(64, 128) for b in blocks], axis=0)
             mixed = product(first, split(block), ((1,), (1,)))
             for l in range(2):
                 lanes = slice(128 * l, 128 * l + 128)
@@ -236,10 +242,11 @@
                     reals.append(x * cos_m - y * sin_m)
                     imags.append(jnp.where(lead, extra[cl : cl + 1], y * cos_m + x * sin_m))
                 done.append(jnp.concatenate(reals + imags, axis=0).T)
-        for bl in range(2):
-            parts = [d[64 * bl : 64 * bl + 64].reshape(4, 1, 16, 128) for d in done]
-            block = jnp.concatenate(parts, axis=1).reshape(256, 128)
-            out[pl.ds(field * 2 + bl, 256, stride=6), :] = block
+        for l in range(2):
+            for bl in range(2):
+                parts = [d[64 * bl : 64 * bl + 64].reshape(4, 1, 16, 128) for d in done[l::2]]
+                block = jnp.concatenate(parts, axis=1).reshape(128, 128)
+                out[pl.ds(6 * l + field * 2 + bl, 128, stride=12), :] = block
 
 
 VMEM = pl.BlockSpec(memory_space=pltpu.VMEM)
@@ -286,7 +293,9 @@
 
 def exchange(x):
     x = x.reshape(256, FIELDS, 2, LANES)
-    x = lax.all_to_all(x, ("rows", "cols"), split_axis=0, concat_axis=0, tiled=True)
+    x = lax.all_to_all(
+        x, ("rows", "cols"), split_axis=0, concat_axis=0, tiled=True, axis_index_groups=[LISTED]
+    )
     return x.reshape(1536, LANES)
 
 

time: 81.1 us -> 78.1 us (0.963)
  blocking collectives: 74.9 us -> 72 us
    all_to_all x2, blocking collectives: 74.9 us -> 72 us  [exchange(): lax.all_to_all(x, ('rows', 'cols'), split_axis=0, concat_axis=0, tiled=Tr...]
where the time goes in v4:
time: 78.1 us; the launch traced here: 78 us
  blocking collectives  72 us (92%)
  Pallas kernels  5.02 us (6%)
  between operations  0.81 us (1%)
    all_to_all x2, blocking collectives, exchange(): lax.all_to_all(x, ('rows', 'cols'), split_axis=0, concat_axis=0, tiled=Tr...  72 us
    pallas_call x3, Pallas kernels, call(): pl.pallas_call(body, out_shape=shapes, in_specs=in_specs, out_specs=out_s...  5.02 us

profile of v4, /device:TPU:1, one launch (start us, length us, event | category | flops | bytes accessed | tf_op | source)
XLA Modules:
  0.0 78.0 jit_solution(5422537563340838138)
XLA Ops:
  0.6 1.4 %shard_map.174 = f32[1536,128]{1,0:T(8,128)S(1)} custom-call(f32[512,128]{1,0:T(8,128)} %bitcast.52, f32[512,128]{1,0:T(8,128)} %bitcast.53, f32[512,128]{1,0:T(8,128)} %bitcast.48, f32[512,128]{1,0:T(8,128)} %bitcast.50), custom_call_target="tpu_custom_call" | custom-call | tf_op jit(solution)/shard_map/pallas_call | solution.py:256
  2.1 0.0 copy-start.2
  2.1 0.0 copy-start.5
  2.1 0.0 copy-start.6
  2.1 0.0 copy-start.7
  2.1 0.0 copy-start.8
  2.1 0.0 copy-start.9
  2.2 0.0 copy-start.10
  2.2 0.0 copy-start.11
  2.2 0.0 copy-start.12
  2.2 40.4 %all_to_all.10 = f32[256,3,2,128]{3,2,1,0:T(2,128)S(1)} all-to-all(f32[256,3,2,128]{3,2,1,0:T(2,128)S(1)} %bitcast.44), channel_id=1, replica_groups={{0,16,8,24,2,18,10,26,4,20,12,28,6,22,14,30,1,17,9,25,3,19,11,27,5,21,1..., dimensions={0} | all-to-all | bytes 1572864 | tf_op jit(solution)/shard_map/all_to_all | solution.py:296
  42.6 0.0 copy-done.2
  42.6 0.0 copy-done.5
  42.7 0.0 copy-done.6
  42.7 0.0 copy-done.7
  42.7 0.0 copy-done.8
  42.7 0.0 copy-done.9
  42.7 0.0 copy-done.10
  42.7 0.0 copy-done.11
  42.7 0.0 copy-done.12
  42.7 2.3 %shard_map.175 = f32[1536,128]{1,0:T(8,128)S(1)} custom-call(f32[1536,128]{1,0:T(8,128)S(1)} %bitcast.45, bf16[144,128]{1,0:T(8,128)(2,1)S(1)} %copy-done.9, bf16[144,128]{1,0:T(8,128)(2,1)S(1)} %copy-done.8, bf16[512,128]{1,0:T(8,128)(2,1)S(1)} %copy-done.6, bf16[512,128]{1,0:T(8,128)(2,1)S(1)} %copy-done.5, bf16[96,96]{1,0:T(8,128)(2,1)S(1)} %copy-done.12, ...), custom_call_target="tpu_custom_call" | custom-call | tf_op jit(solution)/shard_map/pallas_call | solution.py:256
  45.0 0.0 copy-start
  45.0 0.0 copy-start.1
  45.0 0.0 copy-start.3
  45.0 0.0 copy-start.4
  45.0 31.6 %all_to_all.11 = f32[256,3,2,128]{3,2,1,0:T(2,128)S(1)} all-to-all(f32[256,3,2,128]{3,2,1,0:T(2,128)S(1)} %bitcast.46), channel_id=1, replica_groups={{0,16,8,24,2,18,10,26,4,20,12,28,6,22,14,30,1,17,9,25,3,19,11,27,5,21,1..., dimensions={0} | all-to-all | bytes 1572864 | tf_op jit(solution)/shard_map/all_to_all | solution.py:296
  76.6 0.0 copy-done
  76.6 0.0 copy-done.1
  76.6 0.0 copy-done.3
  76.6 0.0 copy-done.4
  76.6 1.3 %shard_map.176 = (f32[512,128]{1,0:T(8,128)}, f32[512,128]{1,0:T(8,128)}, f32[512,128]{1,0:T(8,128)}, f32[512,128]{1,0:T(8,128)}) custom-call(f32[1536,128]{1,0:T(8,128)S(1)} %bitcast.47, bf16[512,128]{1,0:T(8,128)(2,1)S(1)} %copy-done.4, bf16[512,128]{1,0:T(8,128)(2,1)S(1)} %copy-done.3, f32[512,128]{1,0:T(8,128)S(1)} %bitcast.49, f32[512,128]{1,0:T(8,128)S(1)} %bitcast.51), custom_call_target="tpu_custom_call" | custom-call | tf_op jit(solution)/shard_map/pallas_call | solution.py:256
Async XLA Ops:
  2.1 40.6 %copy-start.2 = (f32[2,16,16,128]{3,2,1,0:T(8,128)S(1)}, f32[2,16,16,128]{3,2,1,0:T(8,128)}, u32[]{:S(2)}) copy-start(f32[2,16,16,128]{3,2,1,0:T(8,128)} %constant.29.clone.turn_c) | copy-start | bytes 786436
  2.1 40.6 %copy-start.5 = (bf16[512,128]{1,0:T(8,128)(2,1)S(1)}, bf16[512,128]{1,0:T(8,128)(2,1)}, u32[]{:S(2)}) copy-start(bf16[512,128]{1,0:T(8,128)(2,1)} %constant.25.clone.middle_lo) | copy-start | bytes 393220
  2.1 40.5 %copy-start.6 = (bf16[512,128]{1,0:T(8,128)(2,1)S(1)}, bf16[512,128]{1,0:T(8,128)(2,1)}, u32[]{:S(2)}) copy-start(bf16[512,128]{1,0:T(8,128)(2,1)} %constant.24.clone.middle_hi) | copy-start | bytes 393220
  2.1 40.5 %copy-start.7 = (f32[2,48,128]{2,1,0:T(8,128)S(1)}, f32[2,48,128]{2,1,0:T(8,128)}, u32[]{:S(2)}) copy-start(f32[2,48,128]{2,1,0:T(8,128)} %constant.30.clone.turn_x) | copy-start | bytes 147460
  2.1 40.5 %copy-start.8 = (bf16[144,128]{1,0:T(8,128)(2,1)S(1)}, bf16[144,128]{1,0:T(8,128)(2,1)}, u32[]{:S(2)}) copy-start(bf16[144,128]{1,0:T(8,128)(2,1)} %constant.23.clone.first_lo) | copy-start | bytes 110596
  2.1 40.5 %copy-start.9 = (bf16[144,128]{1,0:T(8,128)(2,1)S(1)}, bf16[144,128]{1,0:T(8,128)(2,1)}, u32[]{:S(2)}) copy-start(bf16[144,128]{1,0:T(8,128)(2,1)} %constant.22.clone.first_hi) | copy-start | bytes 110596
  2.2 40.5 %copy-start.10 = (f32[2,24,128]{2,1,0:T(8,128)S(1)}, f32[2,24,128]{2,1,0:T(8,128)}, u32[]{:S(2)}) copy-start(f32[2,24,128]{2,1,0:T(8,128)} %constant.28.clone.turn_m) | copy-start | bytes 73732
  2.2 40.5 %copy-start.11 = (bf16[96,96]{1,0:T(8,128)(2,1)S(1)}, bf16[96,96]{1,0:T(8,128)(2,1)}, u32[]{:S(2)}) copy-start(bf16[96,96]{1,0:T(8,128)(2,1)} %constant.27.clone.extra_lo) | copy-start | bytes 55300
  2.2 40.5 %copy-start.12 = (bf16[96,96]{1,0:T(8,128)(2,1)S(1)}, bf16[96,96]{1,0:T(8,128)(2,1)}, u32[]{:S(2)}) copy-start(bf16[96,96]{1,0:T(8,128)(2,1)} %constant.26.clone.extra_hi) | copy-start | bytes 55300
  45.0 31.6 %copy-start = (f32[32,2,4,256]{3,2,1,0:T(4,128)S(1)}, f32[32,2,4,256]{3,2,1,0:T(4,128)}, u32[]{:S(2)}) copy-start(f32[32,2,4,256]{3,2,1,0:T(4,128)} %param.17) | copy-start | bytes 786436
  45.0 31.6 %copy-start.1 = (f32[32,2,4,256]{3,2,1,0:T(4,128)S(1)}, f32[32,2,4,256]{3,2,1,0:T(4,128)}, u32[]{:S(2)}) copy-start(f32[32,2,4,256]{3,2,1,0:T(4,128)} %param.18) | copy-start | bytes 786436
  45.0 31.6 %copy-start.3 = (bf16[512,128]{1,0:T(8,128)(2,1)S(1)}, bf16[512,128]{1,0:T(8,128)(2,1)}, u32[]{:S(2)}) copy-start(bf16[512,128]{1,0:T(8,128)(2,1)} %constant.32.clone.last_lo) | copy-start | bytes 393220
  45.0 31.6 %copy-start.4 = (bf16[512,128]{1,0:T(8,128)(2,1)S(1)}, bf16[512,128]{1,0:T(8,128)(2,1)}, u32[]{:S(2)}) copy-start(bf16[512,128]{1,0:T(8,128)(2,1)} %constant.31.clone.last_hi) | copy-start | bytes 393220

commit v5 on v4

--- a/solution.py
+++ b/solution.py
@@ -77,7 +77,7 @@
     turn_x = np.tile(turn_c[:, :, 16], (1, FIELDS, 1))
     turn_c = np.ascontiguousarray(turn_c[:, :, :16])
     return (
-        *halves(first), *halves(tall(middle)), *halves(extra), turn_m, turn_c, turn_x, *halves(tall(last))
+        *halves(first), *halves(tall(middle)), *halves(tall(middle.T)), *halves(extra), *halves(extra.T), turn_m, turn_c, turn_x, *halves(tall(last))
     )
 
 
@@ -163,7 +163,8 @@
 
 
 def channel_kernel(
-    arrived, first_hi, first_lo, middle_hi, middle_lo, extra_hi, extra_lo, turn_m, turn_c, turn_x, out, data,
+    arrived, first_hi, first_lo, middle_hi, middle_lo, inverse_hi, inverse_lo, extra_hi, extra_lo, back_hi, back_lo, turn_m, turn_c, turn_x,
+    out, data,
 ):
     re, im = slice(0, 128), slice(128, 256)
     cos_m, sin_m = turn_m[0, 0:16], turn_m[1, 0:16]
@@ -190,12 +191,11 @@
                 data[rows, re] = x * cos_x
                 data[rows, im] = -(x * sin_x)
 
-    middle = [jnp.concatenate([ref[0:256, :], ref[256:512, :]], axis=1) for ref in (middle_hi, middle_lo)]
-
-    def along_lanes(dims):
+    def along_lanes(refs):
+        table = [jnp.concatenate([ref[0:256, :], ref[256:512, :]], axis=1) for ref in refs]
         for start in range(0, ROWS, CHUNK):
             rows = pl.ds(start, min(CHUNK, ROWS - start))
-            data[rows, :] = product(split(data[rows, :]), middle, dims)
+            data[rows, :] = product(split(data[rows, :]), table, ((1,), (0,)))
 
     def multiply(spectra):
         signal, kernel, grad = spectra
@@ -205,7 +205,7 @@
             [times_conj(g, s) for g, s in zip(grad, signal)],
         )
 
-    along_lanes(((1,), (0,)))
+    along_lanes((middle_hi, middle_lo))
     for start in (0, 8):
         turn = [(turn_c[0, c, start : start + 8], turn_c[1, c, start : start + 8]) for c in range(16)]
         spectra = []
@@ -224,9 +224,9 @@
     spectra = [[(values[16 * f : 16 * f + 16], values[48 + 16 * f : 64 + 16 * f])] for f in range(FIELDS)]
     results = multiply(spectra)
     values = jnp.concatenate([result[0][part] for part in range(2) for result in results], axis=0)
-    values = product(extra, split(values), ((0,), (0,)))
+    values = product((back_hi[...], back_lo[...]), split(values), ((1,), (0,)))
     data[rows, re], data[rows, im] = times((values[:48], values[48:]), turn)
-    along_lanes(((1,), (1,)))
+    along_lanes((inverse_hi, inverse_lo))
 
     lead = lax.broadcasted_iota(jnp.int32, (16, 128), 0) == 0
     for field in range(FIELDS):

time: 78.1 us -> 78.2 us (level)
  no operation moved by 1% of the time
where the time goes in v5:
time: 78.2 us; the launch traced here: 78 us
  blocking collectives  72 us (92%)
  Pallas kernels  5 us (6%)
  between operations  0.87 us (1%)
    all_to_all x2, blocking collectives, exchange(): lax.all_to_all(x, ('rows', 'cols'), split_axis=0, concat_axis=0, tiled=Tr...  72 us
    pallas_call x3, Pallas kernels, call(): pl.pallas_call(body, out_shape=shapes, in_specs=in_specs, out_specs=out_s...  5 us

profile of v5, /device:TPU:1, one launch (start us, length us, event | category | flops | bytes accessed | tf_op | source)
XLA Modules:
  0.0 78.0 jit_solution(4981540386099216022)
XLA Ops:
  0.6 1.4 %shard_map.210 = f32[1536,128]{1,0:T(8,128)S(1)} custom-call(f32[512,128]{1,0:T(8,128)} %bitcast.52, f32[512,128]{1,0:T(8,128)} %bitcast.53, f32[512,128]{1,0:T(8,128)} %bitcast.48, f32[512,128]{1,0:T(8,128)} %bitcast.50), custom_call_target="tpu_custom_call" | custom-call | tf_op jit(solution)/shard_map/pallas_call | solution.py:256
  2.1 0.0 copy-start.2
  2.1 0.0 copy-start.5
  2.1 0.0 copy-start.6
  2.1 0.0 copy-start.7
  2.1 0.0 copy-start.8
  2.1 0.0 copy-start.9
  2.2 0.0 copy-start.10
  2.2 0.0 copy-start.11
  2.2 0.0 copy-start.12
  2.2 0.0 copy-start.13
  2.2 0.0 copy-start.14
  2.2 0.0 copy-start.15
  2.2 0.0 copy-start.16
  2.3 40.4 %all_to_all.10 = f32[256,3,2,128]{3,2,1,0:T(2,128)S(1)} all-to-all(f32[256,3,2,128]{3,2,1,0:T(2,128)S(1)} %bitcast.44), channel_id=1, replica_groups={{0,16,8,24,2,18,10,26,4,20,12,28,6,22,14,30,1,17,9,25,3,19,11,27,5,21,1..., dimensions={0} | all-to-all | bytes 1572864 | tf_op jit(solution)/shard_map/all_to_all | solution.py:296
  42.7 0.0 copy-done.2
  42.7 0.0 copy-done.5
  42.7 0.0 copy-done.6
  42.7 0.0 copy-done.7
  42.7 0.0 copy-done.8
  42.7 0.0 copy-done.9
  42.7 0.0 copy-done.10
  42.7 0.0 copy-done.11
  42.8 0.0 copy-done.12
  42.8 0.0 copy-done.13
  42.8 0.0 copy-done.14
  42.8 0.0 copy-done.15
  42.8 0.0 copy-done.16
  42.8 2.2 %shard_map.211 = f32[1536,128]{1,0:T(8,128)S(1)} custom-call(f32[1536,128]{1,0:T(8,128)S(1)} %bitcast.46, bf16[144,128]{1,0:T(8,128)(2,1)S(1)} %copy-done.11, bf16[144,128]{1,0:T(8,128)(2,1)S(1)} %copy-done.10, bf16[512,128]{1,0:T(8,128)(2,1)S(1)} %copy-done.8, bf16[512,128]{1,0:T(8,128)(2,1)S(1)} %copy-done.7, bf16[512,128]{1,0:T(8,128)(2,1)S(1)} %copy-done.6, ...), custom_call_target="tpu_custom_call" | custom-call | tf_op jit(solution)/shard_map/pallas_call | solution.py:256
  45.1 0.0 copy-start
  45.1 0.0 copy-start.1
  45.1 0.0 copy-start.3
  45.1 0.0 copy-start.4
  45.1 31.6 %all_to_all.11 = f32[256,3,2,128]{3,2,1,0:T(2,128)S(1)} all-to-all(f32[256,3,2,128]{3,2,1,0:T(2,128)S(1)} %bitcast.47), channel_id=1, replica_groups={{0,16,8,24,2,18,10,26,4,20,12,28,6,22,14,30,1,17,9,25,3,19,11,27,5,21,1..., dimensions={0} | all-to-all | bytes 1572864 | tf_op jit(solution)/shard_map/all_to_all | solution.py:296
  76.7 0.0 copy-done
  76.7 0.0 copy-done.1
  76.7 0.0 copy-done.3
  76.7 0.0 copy-done.4
  76.7 1.3 %shard_map.212 = (f32[512,128]{1,0:T(8,128)}, f32[512,128]{1,0:T(8,128)}, f32[512,128]{1,0:T(8,128)}, f32[512,128]{1,0:T(8,128)}) custom-call(f32[1536,128]{1,0:T(8,128)S(1)} %bitcast.45, bf16[512,128]{1,0:T(8,128)(2,1)S(1)} %copy-done.4, bf16[512,128]{1,0:T(8,128)(2,1)S(1)} %copy-done.3, f32[512,128]{1,0:T(8,128)S(1)} %bitcast.49, f32[512,128]{1,0:T(8,128)S(1)} %bitcast.51), custom_call_target="tpu_custom_call" | custom-call | tf_op jit(solution)/shard_map/pallas_call | solution.py:256
Async XLA Ops:
  2.1 40.6 %copy-start.2 = (f32[2,16,16,128]{3,2,1,0:T(8,128)S(1)}, f32[2,16,16,128]{3,2,1,0:T(8,128)}, u32[]{:S(2)}) copy-start(f32[2,16,16,128]{3,2,1,0:T(8,128)} %constant.41.clone.turn_c) | copy-start | bytes 786436
  2.1 40.6 %copy-start.5 = (bf16[512,128]{1,0:T(8,128)(2,1)S(1)}, bf16[512,128]{1,0:T(8,128)(2,1)}, u32[]{:S(2)}) copy-start(bf16[512,128]{1,0:T(8,128)(2,1)} %constant.35.clone.inverse_lo) | copy-start | bytes 393220
  2.1 40.6 %copy-start.6 = (bf16[512,128]{1,0:T(8,128)(2,1)S(1)}, bf16[512,128]{1,0:T(8,128)(2,1)}, u32[]{:S(2)}) copy-start(bf16[512,128]{1,0:T(8,128)(2,1)} %constant.34.clone.inverse_hi) | copy-start | bytes 393220
  2.1 40.6 %copy-start.7 = (bf16[512,128]{1,0:T(8,128)(2,1)S(1)}, bf16[512,128]{1,0:T(8,128)(2,1)}, u32[]{:S(2)}) copy-start(bf16[512,128]{1,0:T(8,128)(2,1)} %constant.33.clone.middle_lo) | copy-start | bytes 393220
  2.1 40.6 %copy-start.8 = (bf16[512,128]{1,0:T(8,128)(2,1)S(1)}, bf16[512,128]{1,0:T(8,128)(2,1)}, u32[]{:S(2)}) copy-start(bf16[512,128]{1,0:T(8,128)(2,1)} %constant.32.clone.middle_hi) | copy-start | bytes 393220
  2.1 40.6 %copy-start.9 = (f32[2,48,128]{2,1,0:T(8,128)S(1)}, f32[2,48,128]{2,1,0:T(8,128)}, u32[]{:S(2)}) copy-start(f32[2,48,128]{2,1,0:T(8,128)} %constant.42.clone.turn_x) | copy-start | bytes 147460
  2.2 40.6 %copy-start.10 = (bf16[144,128]{1,0:T(8,128)(2,1)S(1)}, bf16[144,128]{1,0:T(8,128)(2,1)}, u32[]{:S(2)}) copy-start(bf16[144,128]{1,0:T(8,128)(2,1)} %constant.31.clone.first_lo) | copy-start | bytes 110596
  2.2 40.6 %copy-start.11 = (bf16[144,128]{1,0:T(8,128)(2,1)S(1)}, bf16[144,128]{1,0:T(8,128)(2,1)}, u32[]{:S(2)}) copy-start(bf16[144,128]{1,0:T(8,128)(2,1)} %constant.30.clone.first_hi) | copy-start | bytes 110596
  2.2 40.6 %copy-start.12 = (f32[2,24,128]{2,1,0:T(8,128)S(1)}, f32[2,24,128]{2,1,0:T(8,128)}, u32[]{:S(2)}) copy-start(f32[2,24,128]{2,1,0:T(8,128)} %constant.40.clone.turn_m) | copy-start | bytes 73732
  2.2 40.6 %copy-start.13 = (bf16[96,96]{1,0:T(8,128)(2,1)S(1)}, bf16[96,96]{1,0:T(8,128)(2,1)}, u32[]{:S(2)}) copy-start(bf16[96,96]{1,0:T(8,128)(2,1)} %constant.39.clone.back_lo) | copy-start | bytes 55300
  2.2 40.6 %copy-start.14 = (bf16[96,96]{1,0:T(8,128)(2,1)S(1)}, bf16[96,96]{1,0:T(8,128)(2,1)}, u32[]{:S(2)}) copy-start(bf16[96,96]{1,0:T(8,128)(2,1)} %constant.38.clone.back_hi) | copy-start | bytes 55300
  2.2 40.6 %copy-start.15 = (bf16[96,96]{1,0:T(8,128)(2,1)S(1)}, bf16[96,96]{1,0:T(8,128)(2,1)}, u32[]{:S(2)}) copy-start(bf16[96,96]{1,0:T(8,128)(2,1)} %constant.37.clone.extra_lo) | copy-start | bytes 55300
  2.2 40.6 %copy-start.16 = (bf16[96,96]{1,0:T(8,128)(2,1)S(1)}, bf16[96,96]{1,0:T(8,128)(2,1)}, u32[]{:S(2)}) copy-start(bf16[96,96]{1,0:T(8,128)(2,1)} %constant.36.clone.extra_hi) | copy-start | bytes 55300
  45.1 31.6 %copy-start = (f32[32,2,4,256]{3,2,1,0:T(4,128)S(1)}, f32[32,2,4,256]{3,2,1,0:T(4,128)}, u32[]{:S(2)}) copy-start(f32[32,2,4,256]{3,2,1,0:T(4,128)} %param.21) | copy-start | bytes 786436
  45.1 31.6 %copy-start.1 = (f32[32,2,4,256]{3,2,1,0:T(4,128)S(1)}, f32[32,2,4,256]{3,2,1,0:T(4,128)}, u32[]{:S(2)}) copy-start(f32[32,2,4,256]{3,2,1,0:T(4,128)} %param.22) | copy-start | bytes 786436
  45.1 31.6 %copy-start.3 = (bf16[512,128]{1,0:T(8,128)(2,1)S(1)}, bf16[512,128]{1,0:T(8,128)(2,1)}, u32[]{:S(2)}) copy-start(bf16[512,128]{1,0:T(8,128)(2,1)} %constant.44.clone.last_lo) | copy-start | bytes 393220
  45.1 31.6 %copy-start.4 = (bf16[512,128]{1,0:T(8,128)(2,1)S(1)}, bf16[512,128]{1,0:T(8,128)(2,1)}, u32[]{:S(2)}) copy-start(bf16[512,128]{1,0:T(8,128)(2,1)} %constant.43.clone.last_hi) | copy-start | bytes 393220

commit v6 on v5

--- a/solution.py
+++ b/solution.py
@@ -12,10 +12,10 @@
 LENGTH = 65536
 LISTED = [
     (2 * z + l) * 16 + 8 * h + 2 * x + core
+    for h in range(2)
     for z in range(8)
     for core in range(2)
     for x in range(4)
-    for h in range(2)
     for l in range(2)
 ]
 LANES = 128
@@ -57,8 +57,8 @@
     last = np.stack([np.kron([1.0, 0.0], last), np.kron([0.0, 1.0], last)]).transpose(2, 0, 1, 3).reshape(256, 256)
     first = first.reshape(144, 4, 2, 16).transpose(0, 3, 2, 1).reshape(144, 128)
     lane = np.arange(128)
-    q = 8 * (lane % 2) + 2 * (lane // 2 % 4) + lane // 8 % 2
-    m = 8 * q + 4 * (lane // 64) + lane // 16 % 4
+    q = 8 * (lane // 32 % 2) + 2 * (lane % 4) + lane // 4 % 2
+    m = 8 * q + 4 * (lane // 64) + lane // 8 % 4
     g0 = np.arange(128)
     angle = 2.0 * np.pi * (m[:, None] * g0[None, :] % 128) / 128.0
     middle = np.block([[np.cos(angle), -np.sin(angle)], [np.sin(angle), np.cos(angle)]])
@@ -172,7 +172,7 @@
     first = (first_hi[...], first_lo[...])
     for field in range(FIELDS):
         blocks = [
-            arrived[pl.ds(6 * l + field * 2 + bl, 128, stride=12), :].reshape(4, 2, 16, 128)
+            arrived[pl.ds(6 * l + field * 2 + bl, 128, stride=12), :].reshape(8, 2, 8, 128)
             for l in range(2)
             for bl in range(2)
         ]
@@ -244,7 +244,7 @@
                 done.append(jnp.concatenate(reals + imags, axis=0).T)
         for l in range(2):
             for bl in range(2):
-                parts = [d[64 * bl : 64 * bl + 64].reshape(4, 1, 16, 128) for d in done[l::2]]
+                parts = [d[64 * bl : 64 * bl + 64].reshape(8, 1, 8, 128) for d in done[l::2]]
                 block = jnp.concatenate(parts, axis=1).reshape(128, 128)
                 out[pl.ds(6 * l + field * 2 + bl, 128, stride=12), :] = block
 

time: 78.2 us -> 78.2 us (level)
  no operation moved by 1% of the time
where the time goes in v6:
time: 78.2 us; the launch traced here: 78 us
  blocking collectives  72.1 us (92%)
  Pallas kernels  5 us (6%)
  between operations  0.87 us (1%)
    all_to_all x2, blocking collectives, exchange(): lax.all_to_all(x, ('rows', 'cols'), split_axis=0, concat_axis=0, tiled=Tr...  72.1 us
    pallas_call x3, Pallas kernels, call(): pl.pallas_call(body, out_shape=shapes, in_specs=in_specs, out_specs=out_s...  5 us

profile of v6, /device:TPU:1, one launch (start us, length us, event | category | flops | bytes accessed | tf_op | source)
XLA Modules:
  0.0 78.0 jit_solution(5277564335496235488)
XLA Ops:
  0.6 1.4 %shard_map.210 = f32[1536,128]{1,0:T(8,128)S(1)} custom-call(f32[512,128]{1,0:T(8,128)} %bitcast.52, f32[512,128]{1,0:T(8,128)} %bitcast.53, f32[512,128]{1,0:T(8,128)} %bitcast.48, f32[512,128]{1,0:T(8,128)} %bitcast.50), custom_call_target="tpu_custom_call" | custom-call | tf_op jit(solution)/shard_map/pallas_call | solution.py:256
  2.1 0.0 copy-start.2
  2.1 0.0 copy-start.5
  2.1 0.0 copy-start.6
  2.1 0.0 copy-start.7
  2.1 0.0 copy-start.8
  2.1 0.0 copy-start.9
  2.2 0.0 copy-start.10
  2.2 0.0 copy-start.11
  2.2 0.0 copy-start.12
  2.2 0.0 copy-start.13
  2.2 0.0 copy-start.14
  2.2 0.0 copy-start.15
  2.2 0.0 copy-start.16
  2.3 40.5 %all_to_all.10 = f32[256,3,2,128]{3,2,1,0:T(2,128)S(1)} all-to-all(f32[256,3,2,128]{3,2,1,0:T(2,128)S(1)} %bitcast.44), channel_id=1, replica_groups={{0,16,2,18,4,20,6,22,1,17,3,19,5,21,7,23,32,48,34,50,36,52,38,54,33,49,..., dimensions={0} | all-to-all | bytes 1572864 | tf_op jit(solution)/shard_map/all_to_all | solution.py:296
  42.7 0.0 copy-done.2
  42.7 0.0 copy-done.5
  42.7 0.0 copy-done.6
  42.7 0.0 copy-done.7
  42.7 0.0 copy-done.8
  42.7 0.0 copy-done.9
  42.8 0.0 copy-done.10
  42.8 0.0 copy-done.11
  42.8 0.0 copy-done.12
  42.8 0.0 copy-done.13
  42.8 0.0 copy-done.14
  42.8 0.0 copy-done.15
  42.8 0.0 copy-done.16
  42.8 2.2 %shard_map.211 = f32[1536,128]{1,0:T(8,128)S(1)} custom-call(f32[1536,128]{1,0:T(8,128)S(1)} %bitcast.46, bf16[144,128]{1,0:T(8,128)(2,1)S(1)} %copy-done.11, bf16[144,128]{1,0:T(8,128)(2,1)S(1)} %copy-done.10, bf16[512,128]{1,0:T(8,128)(2,1)S(1)} %copy-done.8, bf16[512,128]{1,0:T(8,128)(2,1)S(1)} %copy-done.7, bf16[512,128]{1,0:T(8,128)(2,1)S(1)} %copy-done.6, ...), custom_call_target="tpu_custom_call" | custom-call | tf_op jit(solution)/shard_map/pallas_call | solution.py:256
  45.1 0.0 copy-start
  45.1 0.0 copy-start.1
  45.1 0.0 copy-start.3
  45.1 0.0 copy-start.4
  45.1 31.6 %all_to_all.11 = f32[256,3,2,128]{3,2,1,0:T(2,128)S(1)} all-to-all(f32[256,3,2,128]{3,2,1,0:T(2,128)S(1)} %bitcast.47), channel_id=1, replica_groups={{0,16,2,18,4,20,6,22,1,17,3,19,5,21,7,23,32,48,34,50,36,52,38,54,33,49,..., dimensions={0} | all-to-all | bytes 1572864 | tf_op jit(solution)/shard_map/all_to_all | solution.py:296
  76.7 0.0 copy-done
  76.7 0.0 copy-done.1
  76.7 0.0 copy-done.3
  76.7 0.0 copy-done.4
  76.7 1.3 %shard_map.212 = (f32[512,128]{1,0:T(8,128)}, f32[512,128]{1,0:T(8,128)}, f32[512,128]{1,0:T(8,128)}, f32[512,128]{1,0:T(8,128)}) custom-call(f32[1536,128]{1,0:T(8,128)S(1)} %bitcast.45, bf16[512,128]{1,0:T(8,128)(2,1)S(1)} %copy-done.4, bf16[512,128]{1,0:T(8,128)(2,1)S(1)} %copy-done.3, f32[512,128]{1,0:T(8,128)S(1)} %bitcast.49, f32[512,128]{1,0:T(8,128)S(1)} %bitcast.51), custom_call_target="tpu_custom_call" | custom-call | tf_op jit(solution)/shard_map/pallas_call | solution.py:256
Async XLA Ops:
  2.1 40.6 %copy-start.2 = (f32[2,16,16,128]{3,2,1,0:T(8,128)S(1)}, f32[2,16,16,128]{3,2,1,0:T(8,128)}, u32[]{:S(2)}) copy-start(f32[2,16,16,128]{3,2,1,0:T(8,128)} %constant.41.clone.turn_c) | copy-start | bytes 786436
  2.1 40.6 %copy-start.5 = (bf16[512,128]{1,0:T(8,128)(2,1)S(1)}, bf16[512,128]{1,0:T(8,128)(2,1)}, u32[]{:S(2)}) copy-start(bf16[512,128]{1,0:T(8,128)(2,1)} %constant.35.clone.inverse_lo) | copy-start | bytes 393220
  2.1 40.6 %copy-start.6 = (bf16[512,128]{1,0:T(8,128)(2,1)S(1)}, bf16[512,128]{1,0:T(8,128)(2,1)}, u32[]{:S(2)}) copy-start(bf16[512,128]{1,0:T(8,128)(2,1)} %constant.34.clone.inverse_hi) | copy-start | bytes 393220
  2.1 40.6 %copy-start.7 = (bf16[512,128]{1,0:T(8,128)(2,1)S(1)}, bf16[512,128]{1,0:T(8,128)(2,1)}, u32[]{:S(2)}) copy-start(bf16[512,128]{1,0:T(8,128)(2,1)} %constant.33.clone.middle_lo) | copy-start | bytes 393220
  2.1 40.6 %copy-start.8 = (bf16[512,128]{1,0:T(8,128)(2,1)S(1)}, bf16[512,128]{1,0:T(8,128)(2,1)}, u32[]{:S(2)}) copy-start(bf16[512,128]{1,0:T(8,128)(2,1)} %constant.32.clone.middle_hi) | copy-start | bytes 393220
  2.1 40.6 %copy-start.9 = (f32[2,48,128]{2,1,0:T(8,128)S(1)}, f32[2,48,128]{2,1,0:T(8,128)}, u32[]{:S(2)}) copy-start(f32[2,48,128]{2,1,0:T(8,128)} %constant.42.clone.turn_x) | copy-start | bytes 147460
  2.2 40.6 %copy-start.10 = (bf16[144,128]{1,0:T(8,128)(2,1)S(1)}, bf16[144,128]{1,0:T(8,128)(2,1)}, u32[]{:S(2)}) copy-start(bf16[144,128]{1,0:T(8,128)(2,1)} %constant.31.clone.first_lo) | copy-start | bytes 110596
  2.2 40.6 %copy-start.11 = (bf16[144,128]{1,0:T(8,128)(2,1)S(1)}, bf16[144,128]{1,0:T(8,128)(2,1)}, u32[]{:S(2)}) copy-start(bf16[144,128]{1,0:T(8,128)(2,1)} %constant.30.clone.first_hi) | copy-start | bytes 110596
  2.2 40.6 %copy-start.12 = (f32[2,24,128]{2,1,0:T(8,128)S(1)}, f32[2,24,128]{2,1,0:T(8,128)}, u32[]{:S(2)}) copy-start(f32[2,24,128]{2,1,0:T(8,128)} %constant.40.clone.turn_m) | copy-start | bytes 73732
  2.2 40.6 %copy-start.13 = (bf16[96,96]{1,0:T(8,128)(2,1)S(1)}, bf16[96,96]{1,0:T(8,128)(2,1)}, u32[]{:S(2)}) copy-start(bf16[96,96]{1,0:T(8,128)(2,1)} %constant.39.clone.back_lo) | copy-start | bytes 55300
  2.2 40.6 %copy-start.14 = (bf16[96,96]{1,0:T(8,128)(2,1)S(1)}, bf16[96,96]{1,0:T(8,128)(2,1)}, u32[]{:S(2)}) copy-start(bf16[96,96]{1,0:T(8,128)(2,1)} %constant.38.clone.back_hi) | copy-start | bytes 55300
  2.2 40.6 %copy-start.15 = (bf16[96,96]{1,0:T(8,128)(2,1)S(1)}, bf16[96,96]{1,0:T(8,128)(2,1)}, u32[]{:S(2)}) copy-start(bf16[96,96]{1,0:T(8,128)(2,1)} %constant.37.clone.extra_lo) | copy-start | bytes 55300
  2.2 40.6 %copy-start.16 = (bf16[96,96]{1,0:T(8,128)(2,1)S(1)}, bf16[96,96]{1,0:T(8,128)(2,1)}, u32[]{:S(2)}) copy-start(bf16[96,96]{1,0:T(8,128)(2,1)} %constant.36.clone.extra_hi) | copy-start | bytes 55300
  45.1 31.6 %copy-start = (f32[32,2,4,256]{3,2,1,0:T(4,128)S(1)}, f32[32,2,4,256]{3,2,1,0:T(4,128)}, u32[]{:S(2)}) copy-start(f32[32,2,4,256]{3,2,1,0:T(4,128)} %param.21) | copy-start | bytes 786436
  45.1 31.6 %copy-start.1 = (f32[32,2,4,256]{3,2,1,0:T(4,128)S(1)}, f32[32,2,4,256]{3,2,1,0:T(4,128)}, u32[]{:S(2)}) copy-start(f32[32,2,4,256]{3,2,1,0:T(4,128)} %param.22) | copy-start | bytes 786436
  45.1 31.6 %copy-start.3 = (bf16[512,128]{1,0:T(8,128)(2,1)S(1)}, bf16[512,128]{1,0:T(8,128)(2,1)}, u32[]{:S(2)}) copy-start(bf16[512,128]{1,0:T(8,128)(2,1)} %constant.44.clone.last_lo) | copy-start | bytes 393220
  45.1 31.6 %copy-start.4 = (bf16[512,128]{1,0:T(8,128)(2,1)S(1)}, bf16[512,128]{1,0:T(8,128)(2,1)}, u32[]{:S(2)}) copy-start(bf16[512,128]{1,0:T(8,128)(2,1)} %constant.43.clone.last_hi) | copy-start | bytes 393220

commit v7 on v5

--- a/solution.py
+++ b/solution.py
@@ -22,7 +22,7 @@
 FIELDS = 3
 EXTRA = 768
 ROWS = EXTRA + 48
-CHUNK = 448
+CHUNK = 480
 SCALE = 1.0 / (65536.0 * 256.0)
 HALF = jnp.bfloat16
 

time: 78.2 us -> 78.2 us (level)
  no operation moved by 1% of the time
where the time goes in v7:
time: 78.2 us; the launch traced here: 78 us
  blocking collectives  72 us (92%)
  Pallas kernels  4.97 us (6%)
  between operations  0.88 us (1%)
    all_to_all x2, blocking collectives, exchange(): lax.all_to_all(x, ('rows', 'cols'), split_axis=0, concat_axis=0, tiled=Tr...  72 us
    pallas_call x3, Pallas kernels, call(): pl.pallas_call(body, out_shape=shapes, in_specs=in_specs, out_specs=out_s...  4.97 us

profile of v7, /device:TPU:1, one launch (start us, length us, event | category | flops | bytes accessed | tf_op | source)
XLA Modules:
  0.0 78.0 jit_solution(16952100191829336293)
XLA Ops:
  0.6 1.4 %shard_map.210 = f32[1536,128]{1,0:T(8,128)S(1)} custom-call(f32[512,128]{1,0:T(8,128)} %bitcast.52, f32[512,128]{1,0:T(8,128)} %bitcast.53, f32[512,128]{1,0:T(8,128)} %bitcast.48, f32[512,128]{1,0:T(8,128)} %bitcast.50), custom_call_target="tpu_custom_call" | custom-call | tf_op jit(solution)/shard_map/pallas_call | solution.py:256
  2.1 0.0 copy-start.2
  2.1 0.0 copy-start.5
  2.1 0.0 copy-start.6
  2.1 0.0 copy-start.7
  2.1 0.0 copy-start.8
  2.1 0.0 copy-start.9
  2.2 0.0 copy-start.10
  2.2 0.0 copy-start.11
  2.2 0.0 copy-start.12
  2.2 0.0 copy-start.13
  2.2 0.0 copy-start.14
  2.2 0.0 copy-start.15
  2.2 0.0 copy-start.16
  2.3 40.4 %all_to_all.10 = f32[256,3,2,128]{3,2,1,0:T(2,128)S(1)} all-to-all(f32[256,3,2,128]{3,2,1,0:T(2,128)S(1)} %bitcast.44), channel_id=1, replica_groups={{0,16,8,24,2,18,10,26,4,20,12,28,6,22,14,30,1,17,9,25,3,19,11,27,5,21,1..., dimensions={0} | all-to-all | bytes 1572864 | tf_op jit(solution)/shard_map/all_to_all | solution.py:296
  42.7 0.0 copy-done.2
  42.7 0.0 copy-done.5
  42.7 0.0 copy-done.6
  42.7 0.0 copy-done.7
  42.7 0.0 copy-done.8
  42.7 0.0 copy-done.9
  42.7 0.0 copy-done.10
  42.7 0.0 copy-done.11
  42.8 0.0 copy-done.12
  42.8 0.0 copy-done.13
  42.8 0.0 copy-done.14
  42.8 0.0 copy-done.15
  42.8 0.0 copy-done.16
  42.8 2.2 %shard_map.211 = f32[1536,128]{1,0:T(8,128)S(1)} custom-call(f32[1536,128]{1,0:T(8,128)S(1)} %bitcast.46, bf16[144,128]{1,0:T(8,128)(2,1)S(1)} %copy-done.11, bf16[144,128]{1,0:T(8,128)(2,1)S(1)} %copy-done.10, bf16[512,128]{1,0:T(8,128)(2,1)S(1)} %copy-done.8, bf16[512,128]{1,0:T(8,128)(2,1)S(1)} %copy-done.7, bf16[512,128]{1,0:T(8,128)(2,1)S(1)} %copy-done.6, ...), custom_call_target="tpu_custom_call" | custom-call | tf_op jit(solution)/shard_map/pallas_call | solution.py:256
  45.0 0.0 copy-start
  45.0 0.0 copy-start.1
  45.1 0.0 copy-start.3
  45.1 0.0 copy-start.4
  45.1 31.6 %all_to_all.11 = f32[256,3,2,128]{3,2,1,0:T(2,128)S(1)} all-to-all(f32[256,3,2,128]{3,2,1,0:T(2,128)S(1)} %bitcast.47), channel_id=1, replica_groups={{0,16,8,24,2,18,10,26,4,20,12,28,6,22,14,30,1,17,9,25,3,19,11,27,5,21,1..., dimensions={0} | all-to-all | bytes 1572864 | tf_op jit(solution)/shard_map/all_to_all | solution.py:296
  76.7 0.0 copy-done
  76.7 0.0 copy-done.1
  76.7 0.0 copy-done.3
  76.7 0.0 copy-done.4
  76.7 1.3 %shard_map.212 = (f32[512,128]{1,0:T(8,128)}, f32[512,128]{1,0:T(8,128)}, f32[512,128]{1,0:T(8,128)}, f32[512,128]{1,0:T(8,128)}) custom-call(f32[1536,128]{1,0:T(8,128)S(1)} %bitcast.45, bf16[512,128]{1,0:T(8,128)(2,1)S(1)} %copy-done.4, bf16[512,128]{1,0:T(8,128)(2,1)S(1)} %copy-done.3, f32[512,128]{1,0:T(8,128)S(1)} %bitcast.49, f32[512,128]{1,0:T(8,128)S(1)} %bitcast.51), custom_call_target="tpu_custom_call" | custom-call | tf_op jit(solution)/shard_map/pallas_call | solution.py:256
Async XLA Ops:
  2.1 40.6 %copy-start.2 = (f32[2,16,16,128]{3,2,1,0:T(8,128)S(1)}, f32[2,16,16,128]{3,2,1,0:T(8,128)}, u32[]{:S(2)}) copy-start(f32[2,16,16,128]{3,2,1,0:T(8,128)} %constant.41.clone.turn_c) | copy-start | bytes 786436
  2.1 40.6 %copy-start.5 = (bf16[512,128]{1,0:T(8,128)(2,1)S(1)}, bf16[512,128]{1,0:T(8,128)(2,1)}, u32[]{:S(2)}) copy-start(bf16[512,128]{1,0:T(8,128)(2,1)} %constant.35.clone.inverse_lo) | copy-start | bytes 393220
  2.1 40.6 %copy-start.6 = (bf16[512,128]{1,0:T(8,128)(2,1)S(1)}, bf16[512,128]{1,0:T(8,128)(2,1)}, u32[]{:S(2)}) copy-start(bf16[512,128]{1,0:T(8,128)(2,1)} %constant.34.clone.inverse_hi) | copy-start | bytes 393220
  2.1 40.6 %copy-start.7 = (bf16[512,128]{1,0:T(8,128)(2,1)S(1)}, bf16[512,128]{1,0:T(8,128)(2,1)}, u32[]{:S(2)}) copy-start(bf16[512,128]{1,0:T(8,128)(2,1)} %constant.33.clone.middle_lo) | copy-start | bytes 393220
  2.1 40.6 %copy-start.8 = (bf16[512,128]{1,0:T(8,128)(2,1)S(1)}, bf16[512,128]{1,0:T(8,128)(2,1)}, u32[]{:S(2)}) copy-start(bf16[512,128]{1,0:T(8,128)(2,1)} %constant.32.clone.middle_hi) | copy-start | bytes 393220
  2.1 40.6 %copy-start.9 = (f32[2,48,128]{2,1,0:T(8,128)S(1)}, f32[2,48,128]{2,1,0:T(8,128)}, u32[]{:S(2)}) copy-start(f32[2,48,128]{2,1,0:T(8,128)} %constant.42.clone.turn_x) | copy-start | bytes 147460
  2.2 40.6 %copy-start.10 = (bf16[144,128]{1,0:T(8,128)(2,1)S(1)}, bf16[144,128]{1,0:T(8,128)(2,1)}, u32[]{:S(2)}) copy-start(bf16[144,128]{1,0:T(8,128)(2,1)} %constant.31.clone.first_lo) | copy-start | bytes 110596
  2.2 40.6 %copy-start.11 = (bf16[144,128]{1,0:T(8,128)(2,1)S(1)}, bf16[144,128]{1,0:T(8,128)(2,1)}, u32[]{:S(2)}) copy-start(bf16[144,128]{1,0:T(8,128)(2,1)} %constant.30.clone.first_hi) | copy-start | bytes 110596
  2.2 40.6 %copy-start.12 = (f32[2,24,128]{2,1,0:T(8,128)S(1)}, f32[2,24,128]{2,1,0:T(8,128)}, u32[]{:S(2)}) copy-start(f32[2,24,128]{2,1,0:T(8,128)} %constant.40.clone.turn_m) | copy-start | bytes 73732
  2.2 40.6 %copy-start.13 = (bf16[96,96]{1,0:T(8,128)(2,1)S(1)}, bf16[96,96]{1,0:T(8,128)(2,1)}, u32[]{:S(2)}) copy-start(bf16[96,96]{1,0:T(8,128)(2,1)} %constant.39.clone.back_lo) | copy-start | bytes 55300
  2.2 40.6 %copy-start.14 = (bf16[96,96]{1,0:T(8,128)(2,1)S(1)}, bf16[96,96]{1,0:T(8,128)(2,1)}, u32[]{:S(2)}) copy-start(bf16[96,96]{1,0:T(8,128)(2,1)} %constant.38.clone.back_hi) | copy-start | bytes 55300
  2.2 40.6 %copy-start.15 = (bf16[96,96]{1,0:T(8,128)(2,1)S(1)}, bf16[96,96]{1,0:T(8,128)(2,1)}, u32[]{:S(2)}) copy-start(bf16[96,96]{1,0:T(8,128)(2,1)} %constant.37.clone.extra_lo) | copy-start | bytes 55300
  2.2 40.6 %copy-start.16 = (bf16[96,96]{1,0:T(8,128)(2,1)S(1)}, bf16[96,96]{1,0:T(8,128)(2,1)}, u32[]{:S(2)}) copy-start(bf16[96,96]{1,0:T(8,128)(2,1)} %constant.36.clone.extra_hi) | copy-start | bytes 55300
  45.0 31.6 %copy-start = (f32[32,2,4,256]{3,2,1,0:T(4,128)S(1)}, f32[32,2,4,256]{3,2,1,0:T(4,128)}, u32[]{:S(2)}) copy-start(f32[32,2,4,256]{3,2,1,0:T(4,128)} %param.21) | copy-start | bytes 786436
  45.0 31.6 %copy-start.1 = (f32[32,2,4,256]{3,2,1,0:T(4,128)S(1)}, f32[32,2,4,256]{3,2,1,0:T(4,128)}, u32[]{:S(2)}) copy-start(f32[32,2,4,256]{3,2,1,0:T(4,128)} %param.22) | copy-start | bytes 786436
  45.1 31.6 %copy-start.3 = (bf16[512,128]{1,0:T(8,128)(2,1)S(1)}, bf16[512,128]{1,0:T(8,128)(2,1)}, u32[]{:S(2)}) copy-start(bf16[512,128]{1,0:T(8,128)(2,1)} %constant.44.clone.last_lo) | copy-start | bytes 393220
  45.1 31.6 %copy-start.4 = (bf16[512,128]{1,0:T(8,128)(2,1)S(1)}, bf16[512,128]{1,0:T(8,128)(2,1)}, u32[]{:S(2)}) copy-start(bf16[512,128]{1,0:T(8,128)(2,1)} %constant.43.clone.last_hi) | copy-start | bytes 393220
